TPU v7x, 256 devices: a whole 4x4x8 slice. The times are simulated.
256 devices in a mesh: sub: 64 (over x, z, core), blk: 4 (over y).
Axes of the slice: x: 4, y: 4, z: 8, core: 2. Of those that a mesh axis runs over, the one named last changes fastest.
Arguments:
- slave_blocks: bfloat16 [32768, 4, 512], P(('sub', 'blk')), may hold values from -6 to 6
- masters: int32 [32768, 2], P(('sub', 'blk')), may hold values from 0 to 63, all different within a row; in each aligned block of 128 rows (0 to 127, 128 to 255, ...) at most 8 rows name the same one
- master_weight: float32 [32768, 2], P(('sub', 'blk')), may hold values from 0.3 to 1
- active: int32 [32768], P(('sub', 'blk')), may hold values 0 or 1
- multiplier: float32 [32768, 512], P(('sub', 'blk')), may hold values from -6 to 6
- mortar: bfloat16 [131072, 512], P(('sub', 'blk')), may hold values from -0.25 to 0.25
- schur_rows: bfloat16 [32768, 512], P(('sub', 'blk'))
- patch_coupling: float32 [32768, 512], P(('sub', 'blk'))
- corner_local: int32 [4096], P(('sub', 'blk')), may hold values from 0 to 65535
- corner_global: int32 [4096], P(('sub', 'blk')), may hold values from 0 to 1023
- coarse_inverse: float32 [1024, 1024], replicated
Outputs:
- mortar_blocks: float32 [32768, 4, 512], P(('sub', 'blk'))
- schur_image: float32 [32768, 512], P(('sub', 'blk'))
Inputs may be any that keep to these rules, and one draw needn't show every extreme that they name: The two masters of a patch differ; among the patches of one device no subdomain is named more than 8 times, a bound that some block reaches in every draw.
All inputs are finite; a program needn't handle non-finite values. No bound on the sum of `active` on one device may be relied on, other than what follows from the above.
Results may differ from a plain program's by a relative error of at most 0.0043.
Values may be sent and summed in bfloat16 or wider, within the bound.
A program may use at most 128 MiB of HBM per device.

v0:
```python
import jax
import jax.numpy as jnp
from jax import lax
from jax.sharding import PartitionSpec as P


def with_halo(cells, sides, width):
    for axis, dim in sides:
        count = lax.axis_size(axis)
        ends = count - 1
        head = lax.slice_in_dim(cells, 0, width, axis=dim)
        tail = lax.slice_in_dim(cells, cells.shape[dim] - width, cells.shape[dim], axis=dim)
        cells = jnp.concatenate(
            [
                lax.ppermute(tail, axis, [(i, (i + 1) % count) for i in range(ends)]),
                cells,
                lax.ppermute(head, axis, [((i + 1) % count, i) for i in range(ends)]),
            ],
            axis=dim,
        )
    return cells


def body(
    slave_blocks,
    masters,
    master_weight,
    active,
    multiplier,
    mortar,
    schur_rows,
    patch_coupling,
    corner_local,
    corner_global,
    coarse_inverse,
):
    patch_count = slave_blocks.shape[0]
    node_count = slave_blocks.shape[2]
    subdomains = lax.axis_size("sub")
    capacity = max(2, (4 * patch_count + subdomains - 1) // subdomains)
    destination = masters.reshape(-1)
    one_hot_dest = (
        destination[:, None] == jnp.arange(subdomains, dtype=jnp.int32)[None, :]
    ).astype(jnp.int32)
    earlier = jnp.cumsum(one_hot_dest, axis=0) - one_hot_dest
    slot_rank = jnp.sum(earlier * one_hot_dest, axis=1)
    slot_index = destination * capacity + slot_rank
    doubled = jnp.repeat(slave_blocks.reshape(patch_count, 4 * node_count), 2, axis=0)
    outgoing = (
        jnp.zeros((subdomains * capacity, 4 * node_count), jnp.bfloat16).at[slot_index].set(doubled)
    )
    arrived = lax.all_to_all(
        outgoing.reshape(subdomains, capacity, 4 * node_count),
        "sub",
        split_axis=0,
        concat_axis=0,
        tiled=True,
    )
    product = jnp.dot(
        arrived.reshape(-1, node_count), mortar, preferred_element_type=jnp.float32
    ).astype(jnp.bfloat16)
    returned = lax.all_to_all(
        product.reshape(arrived.shape), "sub", split_axis=0, concat_axis=0, tiled=True
    )
    picked = returned.reshape(subdomains * capacity, 4, node_count)[slot_index].astype(jnp.float32)
    picked = picked.reshape(patch_count, 2, 4, node_count)
    mortar_blocks = jnp.sum(master_weight[:, :, None, None] * picked, axis=1)
    normal_gap = mortar_blocks[:, 0]
    magnitude = jnp.sqrt(1.0 + jnp.sum(mortar_blocks[:, 1:] ** 2, axis=1))
    active_flag = active.astype(jnp.float32)[:, None]
    residual = active_flag * normal_gap / magnitude + (1.0 - active_flag) * multiplier
    local_sq = jnp.sum(residual * residual)
    local_count = jnp.sum(active.astype(jnp.float32))
    rounded = residual.astype(jnp.bfloat16)
    columns = rounded
    reduced = jnp.dot(
        columns,
        lax.all_gather(schur_rows, "blk", axis=0, tiled=True),
        preferred_element_type=jnp.float32,
    ).astype(jnp.bfloat16)
    columns = patch_coupling
    applied = jnp.dot(
        columns,
        lax.all_gather(reduced, "blk", axis=0, tiled=True).astype(jnp.float32),
        precision=lax.Precision.HIGHEST,
    )
    padded = with_halo(rounded, (("sub", 0),), patch_count)
    before = padded[:patch_count].astype(jnp.float32)
    following = padded[2 * patch_count :].astype(jnp.float32)
    flat_image = (applied - 0.25 * (before + following)).reshape(-1)
    corner_total = coarse_inverse.shape[0]
    member = (corner_global[:, None] == jnp.arange(corner_total, dtype=jnp.int32)[None, :]).astype(
        jnp.float32
    )
    total_sq, total_count = lax.psum((local_sq, local_count), ("sub", "blk"))
    scale_factor = jnp.sqrt(total_count * node_count / (total_sq + 1e-06))
    scaled_field = scale_factor * flat_image
    picked_values = jnp.take(scaled_field, corner_local)
    assembled = lax.psum(
        jnp.dot(picked_values, member, precision=lax.Precision.HIGHEST), ("sub", "blk")
    )
    final_factor = jnp.float32(1.0)
    coarse = jnp.dot(coarse_inverse, assembled, precision=lax.Precision.HIGHEST)
    spread_back = jnp.dot(member, coarse, precision=lax.Precision.HIGHEST)
    corrected = scaled_field.at[corner_local].add(spread_back)
    schur_image = (final_factor * corrected).reshape(patch_count, node_count)
    return (mortar_blocks, schur_image)


def solution(mesh):
    in_specs = (
        P(("sub", "blk"), None, None),
        P(("sub", "blk"), None),
        P(("sub", "blk"), None),
        P(("sub", "blk")),
        P(("sub", "blk"), None),
        P(("sub", "blk"), None),
        P(("sub", "blk"), None),
        P(("sub", "blk"), None),
        P(("sub", "blk")),
        P(("sub", "blk")),
        P(),
    )
    out_specs = (P(("sub", "blk"), None, None), P(("sub", "blk"), None))
    return jax.shard_map(body, mesh=mesh, in_specs=in_specs, out_specs=out_specs, check_vma=False)
```

profile of v0, /device:TPU:1, one launch (start us, length us, event | category | flops | bytes accessed | tf_op | source)
XLA Modules:
  0.0 328.5 jit_solution(15650741098329437902)
XLA Ops:
  0.6 0.8 copy.34
  1.8 0.7 broadcast_multiply_fusion
  2.5 0.6 reduce-window.6
  3.6 1.1 copy.43
  4.7 0.6 broadcast_in_dim.8
  5.4 1.2 reshape.117
  6.7 3.5 %scatter_custom_fusion = bf16[512,2048]{1,0:T(8,128)(2,1)S(1)} fusion(s32[256]{0:T(256)S(1)} %bitcast.65, bf16[256,2048]{1,0:T(8,128)(2,1)} %reshape.117, bf16[]{:T(256)} %constant.12.clone.1), kind=kCustom, calls=%fused_computation.13 | custom fusion | bytes 2097664 | tf_op jit(solution)/shard_map/scatter | solution.py:50
  10.2 64.1 %all_to_all.10 = bf16[64,8,2048]{2,1,0:T(8,128)(2,1)} all-to-all(bf16[64,8,2048]{2,1,0:T(8,128)(2,1)S(1)} %bitcast.59), channel_id=1, replica_groups=mesh['sub'=64,'blk'=4] {'sub'}, dimensions={0} | all-to-all | bytes 4194304 | tf_op jit(solution)/shard_map/all_to_all | solution.py:52
  74.3 3.1 reshape.92
  77.4 2.6 convolution_convert_fusion
  80.1 4.4 %reshape.93 = bf16[64,8,2048]{2,1,0:T(8,128)(2,1)} reshape(bf16[2048,512]{1,0:T(8,128)(2,1)} %convolution_convert_fusion) | data formatting | bytes 4194304 | tf_op jit(solution)/shard_map/reshape | solution.py:63
  84.4 6.0 %all-to-all-start.1 = ((bf16[64,8,2048]{2,1,0:T(8,128)(2,1)}), bf16[64,8,2048]{2,1,0:T(8,128)(2,1)S(1)}, u32[]{:S(2)}, u32[]{:S(2)}) async-start(bf16[64,8,2048]{2,1,0:T(8,128)(2,1)} %reshape.93), calls=%async_computation.1 | async-start | bytes 4194304 | tf_op jit(solution)/shard_map/all_to_all | solution.py:62
  90.7 11.8 %all_gather.6 = bf16[512,512]{1,0:T(8,128)(2,1)S(1)} all-gather(bf16[128,512]{1,0:T(8,128)(2,1)} %param.17), channel_id=1, replica_groups=mesh['sub'=64,'blk'=4] {'blk'}, dimensions={0}, use_global_device_ids=true | all-gather | bytes 655360 | tf_op jit(solution)/shard_map/all_gather | solution.py:78
  102.5 0.6 convert_reduce_fusion
  103.1 38.5 %all-to-all-done.1 = bf16[64,8,2048]{2,1,0:T(8,128)(2,1)S(1)} async-done(((bf16[64,8,2048]{2,1,0:T(8,128)(2,1)}), bf16[64,8,2048]{2,1,0:T(8,128)(2,1)S(1)}, u32[]{:S(2)}, u32[]{:S(2)}) %all-to-all-start.1) | async-done | bytes 2097184 | tf_op jit(solution)/shard_map/all_to_all | solution.py:62
  141.6 2.8 reshape.94
  144.4 3.1 gather_fusion
  147.5 1.0 fusion
  148.5 0.8 fusion.1
  149.8 0.8 multiply_reduce_fusion
  150.6 2.1 collective-permute-start
  152.7 2.2 collective-permute-start.1
  154.9 76.5 %all-reduce = (f32[]{:T(128)}, f32[]{:T(128)}) all-reduce(f32[]{:T(128)} %get-tuple-element.10, f32[]{:T(128)} %get-tuple-element.8), channel_id=1, replica_groups=mesh['sub'=64,'blk'=4] {'sub','blk'}, use_global_device_ids=true, to_apply=%region_6.7 | all-reduce | flops 2 | bytes 16 | tf_op jit(solution)/shard_map/psum | solution.py:95
  232.7 0.2 convolution_convert_fusion.1
  233.0 9.9 %all_gather.7 = bf16[512,512]{1,0:T(8,128)(2,1)S(1)} all-gather(bf16[128,512]{1,0:T(8,128)(2,1)S(1)} %convolution_convert_fusion.1), channel_id=1, replica_groups=mesh['sub'=64,'blk'=4] {'blk'}, dimensions={0}, use_global_device_ids=true | all-gather | bytes 655360 | tf_op jit(solution)/shard_map/all_gather | solution.py:84
  242.9 0.7 subtract_multiply_fusion
  243.8 0.7 gather_fusion.1
  244.5 0.2 fusion.9
  244.7 76.4 %psum.23 = f32[1024]{0:T(1024)S(1)} all-reduce(f32[1024]{0:T(1024)S(1)} %bitcast.67), channel_id=1, replica_groups=mesh['sub'=64,'blk'=4] {'sub','blk'}, use_global_device_ids=true, to_apply=%region_10.11 | all-reduce | flops 1024 | bytes 8192 | tf_op jit(solution)/shard_map/psum | solution.py:99
  321.1 5.6 %convolution_bitcast_fusion.1 = f32[1024,1]{0,1:T(1,128)S(1)} fusion(f32[1024,1]{0,1:T(1,128)S(1)} %bitcast.63, f32[1024,1024]{1,0:T(8,128)} %param.21), kind=kOutput, calls=%fused_computation.9 | convolution fusion | flops 12582912 | bytes 4202496 | tf_op jit(solution)/shard_map/dot_general | solution.py:103
  326.9 0.8 scatter_fusion
  327.8 0.7 reshape.95
  (40 shorter events, 2.0 us)
Async XLA Ops:
  0.6 76.8 %copy-start = (bf16[512,512]{1,0:T(8,128)(2,1)S(1)}, bf16[512,512]{1,0:T(8,128)(2,1)}, u32[]{:S(2)}) copy-start(bf16[512,512]{1,0:T(8,128)(2,1)} %param.16) | copy-start | bytes 1572868
  84.4 6.0 %copy-start.4 = (f32[128,2]{0,1:T(2,128)S(1)}, f32[128,2]{0,1:T(2,128)}, u32[]{:S(2)}) copy-start(f32[128,2]{0,1:T(2,128)} %param.13) | copy-start | bytes 3076
  84.4 6.1 %copy-start.3 = (f32[128,512]{1,0:T(8,128)S(1)}, f32[128,512]{1,0:T(8,128)}, u32[]{:S(2)}) copy-start(f32[128,512]{1,0:T(8,128)} %param.15) | copy-start | bytes 786436
  84.4 6.2 %copy-start.5 = (s32[128]{0:T(128)S(1)}, s32[128]{0:T(128)}, u32[]{:S(2)}) copy-start(s32[128]{0:T(128)} %param.14) | copy-start | bytes 1540
  84.4 6.3 %copy-start.6 = (s32[16]{0:T(128)S(1)}, s32[16]{0:T(128)}, u32[]{:S(2)}) copy-start(s32[16]{0:T(128)} %param.19) | copy-start | bytes 196
  84.4 57.2 %all-to-all-start.1 = ((bf16[64,8,2048]{2,1,0:T(8,128)(2,1)}), bf16[64,8,2048]{2,1,0:T(8,128)(2,1)S(1)}, u32[]{:S(2)}, u32[]{:S(2)}) async-start(bf16[64,8,2048]{2,1,0:T(8,128)(2,1)} %reshape.93), calls=%async_computation.1 | async-start | bytes 4194304 | tf_op jit(solution)/shard_map/all_to_all | solution.py:62
  148.5 84.4 %copy-start.1 = (f32[128,4,512]{2,1,0:T(4,128)}, f32[128,4,512]{2,1,0:T(4,128)S(1)}, u32[]{:S(2)}) copy-start(f32[128,4,512]{2,1,0:T(4,128)S(1)} %fusion) | copy-start | bytes 3145732
  149.3 93.5 %copy-start.2 = (f32[128,512]{1,0:T(8,128)S(1)}, f32[128,512]{1,0:T(8,128)}, u32[]{:S(2)}) copy-start(f32[128,512]{1,0:T(8,128)} %param.18) | copy-start | bytes 786436
  150.6 92.3 %collective-permute-start = (bf16[128,512]{0,1:T(8,128)(2,1)S(1)}, bf16[128,512]{0,1:T(8,128)(2,1)S(1)}, u32[]{:S(2)}, u32[]{:S(2)}) collective-permute-start(bf16[128,512]{0,1:T(8,128)(2,1)S(1)} %get-tuple-element.9), channel_id=1, source_target_pairs={{0,4},{4,8},{8,12},{12,16},{16,20},{20,24},{24,28},{28,32},{32,36}... | collective-permute-start | bytes 393224 | tf_op jit(solution)/shard_map/ppermute | solution.py:15
  152.7 90.2 %collective-permute-start.1 = (bf16[128,512]{0,1:T(8,128)(2,1)S(1)}, bf16[128,512]{0,1:T(8,128)(2,1)S(1)}, u32[]{:S(2)}, u32[]{:S(2)}) collective-permute-start(bf16[128,512]{0,1:T(8,128)(2,1)S(1)} %get-tuple-element.9), channel_id=1, source_target_pairs={{4,0},{8,4},{12,8},{16,12},{20,16},{24,20},{28,24},{32,28},{36,32}... | collective-permute-start | bytes 393224 | tf_op jit(solution)/shard_map/ppermute | solution.py:17
  232.7 11.8 %copy-start.7 = (s32[16]{0:T(128)S(1)}, s32[16]{0:T(128)}, u32[]{:S(2)}) copy-start(s32[16]{0:T(128)} %param.20) | copy-start | bytes 196
where the time goes:
time: 329 us
  blocking collectives  239 us (73%)
  waiting for transfers between devices  38.5 us (12%)
  local copies, waits for them, and re-layouts  23.7 us (7%)
  starting transfers between devices  10.3 us (3%)
  matrix products  9.62 us (3%)
  other arithmetic  5.43 us (2%)
    psum x1, blocking collectives, body(): total_sq, total_count = lax.psum((local_sq, local_count), ('sub', 'blk'))  76.5 us
    psum x1, blocking collectives, body(): lax.psum(jnp.dot(picked_values, member, precision=lax.Precision.HIGHEST),...  76.4 us
    all_to_all x1, blocking collectives, body(): lax.all_to_all(outgoing.reshape(subdomains, capacity, 4 * node_count), 's...  64.1 us
    all_to_all x1, waiting for transfers between devices, body(): lax.all_to_all(product.reshape(arrived.shape), 'sub', split_axis=0, conca...  38.5 us
    all_gather x1, blocking collectives, body(): lax.all_gather(schur_rows, 'blk', axis=0, tiled=True)  11.8 us
    all_gather x1, blocking collectives, body(): lax.all_gather(reduced, 'blk', axis=0, tiled=True).astype(jnp.float32)  9.9 us
  transfers between devices with their start and end apart: 3, of which 1 were waited for; matrix products, arithmetic and copies ran while one was open for 0% of the time, Pallas kernels for 0%

commit v1 on v0

v1 whole, which is shorter than its diff:
```python
import functools

import jax
import jax.numpy as jnp
from jax import lax
from jax.experimental import pallas as pl
from jax.experimental.pallas import tpu as pltpu
from jax.sharding import PartitionSpec as P

NX, NZ, NB = 4, 8, 4
PATCH = 128
NODE = 512
CORNERS = 16
COARSE = 1024
MESSAGE = COARSE + 128
MESH = pl.DeviceIdType.MESH
F32, BF16, I32 = jnp.float32, jnp.bfloat16, jnp.int32


def iota(shape, dim):
    return lax.broadcasted_iota(I32, shape, dim)


def dot(a, b):
    return jnp.dot(a, b, preferred_element_type=F32)


def column(row):
    n = row.shape[1]
    return jnp.sum(jnp.where(iota((n, n), 0) == iota((n, n), 1), row, 0.0), axis=1, keepdims=True)


def split3(a):
    high = a.astype(BF16)
    rest = a - high.astype(F32)
    middle = rest.astype(BF16)
    low = (rest - middle.astype(F32)).astype(BF16)
    return high, middle, low


def kernel(
    slave,
    masters,
    weight,
    active,
    multiplier,
    mortar,
    schur,
    coupling,
    corner_local,
    corner_global,
    corner_global_s,
    coarse_inverse,
    blocks_out,
    image_out,
    table,
    rows,
    names,
    packed,
    product,
    returned,
    factor,
    reduced,
    halo,
    sum_a,
    sum_b,
    inverse,
    inverse_rows,
    t_send,
    t_recv,
    s_send,
    s_recv,
    n_send,
    n_recv,
    r_send,
    r_recv,
    y_send,
    y_recv,
    h_send,
    h_recv,
    a_send,
    a_recv,
    b_send,
    b_recv,
    local_sem,
):
    sub = lax.axis_index("sub")
    blk = lax.axis_index("blk")
    x = sub // (2 * NZ)
    z = (sub // 2) % NZ
    core = sub % 2

    def at(dx=0, dz=0, dc=0, dy=0):
        xx = (x + dx) % NX
        zz = (z + dz) % NZ
        return ((xx * NZ + zz) * 2 + (core + dc) % 2, (blk + dy) % NB)

    sends = []

    def send(src, dst, send_sem, recv_sem, to):
        copy = pltpu.make_async_remote_copy(
            src_ref=src,
            dst_ref=dst,
            send_sem=send_sem,
            recv_sem=recv_sem,
            device_id=to,
            device_id_type=MESH,
        )
        copy.start()
        sends.append(copy)
        return copy

    load_inverse = pltpu.make_async_copy(coarse_inverse, inverse, local_sem.at[0])
    load_inverse.start()

    row_peers = [(dx, dc) for dx in range(NX) for dc in range(2)]
    group_a = [(dx, dy) for dx in range(NX) for dy in range(NB)]
    group_b = [(dz, dc) for dz in range(NZ) for dc in range(2)]
    greet = {(dx, 0, dc, 0) for dx, dc in row_peers}
    greet |= {(dx, 0, 0, dy) for dx, dy in group_a}
    greet |= {(0, dz, dc, 0) for dz, dc in group_b}
    greet = sorted(greet - {(0, 0, 0, 0)})
    before, behind = ((sub + 63) % 64, blk), ((sub + 1) % 64, blk)
    barrier = pltpu.get_barrier_semaphore()
    for dx, dz, dc, dy in greet:
        pl.semaphore_signal(barrier, inc=1, device_id=at(dx, dz, dc, dy), device_id_type=MESH)
    for neighbour in (before, behind):
        pl.semaphore_signal(barrier, inc=1, device_id=neighbour, device_id_type=MESH)
    names[0] = jnp.zeros((8, PATCH), I32)
    names[0, 0:2, :] = masters[...]
    pl.semaphore_wait(barrier, len(greet) + 2)

    def half(ref, h):
        return ref.at[pl.ds(h * 256, 256)]

    tables = {}

    def send_table(way, step, h):
        slot = (-step) % NZ if way == 0 else step
        land = (-step - 1) % NZ if way == 0 else step + 1
        src = mortar if step == 0 else table.at[slot]
        tables[way, step, h] = send(
            half(src, h),
            half(table.at[land], h),
            t_send.at[way, step, h],
            t_recv.at[way, step, h],
            at(dz=1 if way == 0 else -1),
        )

    def pass_tables(step, turn):
        for way in (0, 1):
            h = turn if way == 0 else 1 - turn
            tables[way, step, h].wait_recv()
            if step < 2 or (step == 2 and turn == 0):
                send_table(way, step + 1, h)

    for turn in (0, 1):
        send_table(0, 0, turn)
        send_table(1, 0, 1 - turn)

    names_copies = [
        send(
            names.at[0],
            names.at[((-dx) % NX) * 2 + dc],
            n_send.at[dx * 2 + dc],
            n_recv.at[((-dx) % NX) * 2 + dc],
            at(dx=dx, dc=dc),
        )
        for dx, dc in row_peers[1:]
    ]

    def pair(slot, h):
        return rows.at[slot, pl.ds(2 * h, 2)]

    own = [slave.at[pl.ds(0, 2)], slave.at[pl.ds(2, 2)]]
    s_copy = {}

    def send_rows(key, number, src, dst, to):
        s_copy[key] = send(src, dst, s_send.at[number], s_recv.at[number], to)

    send_rows("up0", 0, own[0], pair(6, 0), at(dx=1))
    send_rows("down1", 1, own[1], pair(2, 1), at(dx=-1))
    send_rows("up1", 2, own[1], pair(6, 1), at(dx=1))
    send_rows("down0", 3, own[0], pair(2, 0), at(dx=-1))
    send_rows("side0", 4, own[0], pair(1, 0), at(dc=1))
    send_rows("side1", 5, own[1], pair(1, 1), at(dc=1))

    factor_copies = []
    own_rows = pl.ds(pl.multiple_of(blk * PATCH, PATCH), PATCH)
    for dy in range(1, NB):
        factor_copies.append(
            send(schur, factor.at[own_rows], y_send.at[0, dy], y_recv.at[0, dy], at(dy=dy))
        )
    own_factor = pltpu.make_async_copy(schur, factor.at[own_rows], local_sem.at[1])
    own_factor.start()

    strict = (iota((256, 256), 0) < iota((256, 256), 1)).astype(F32).astype(BF16)

    def entries(name):
        return jnp.concatenate([name[0:1, :], name[1:2, :]], axis=1)

    own_entries = entries(masters[...])
    named = (own_entries == iota((64, 256), 0)).astype(F32)
    rank = jnp.sum(named * dot(named.astype(BF16), strict), axis=0, keepdims=True)
    ez, ex, ec = (own_entries // 2) % NZ, own_entries // (2 * NZ), own_entries % 2
    place = ((ez - z + NZ) % NZ) * 256 + (((ex - x + NX) % NX) * 2 + (ec + core) % 2) * 32
    place = place.astype(F32) + rank
    codes = [column(place[:, j * PATCH : (j + 1) * PATCH]) for j in range(2)]
    weights = [column(weight[j : j + 1, :]) for j in range(2)]

    for copy in names_copies:
        copy.wait_recv()
    mine = ((x * NZ + (z + iota((8, 256), 0)) % NZ) * 2 + core).astype(I32)
    named = jnp.concatenate(
        [(entries(names[slot]) == mine).astype(F32) for slot in range(8)], axis=0
    )
    ranks = jnp.where(named > 0.0, dot(named.astype(BF16), strict), -1.0)
    wanted = iota((8, 256), 0).astype(F32)

    def pack(slot):
        picks = []
        for d in range(NZ):
            line = ranks[slot * 8 + d : slot * 8 + d + 1, :]
            hit = (line == wanted).astype(F32)
            picks.append(hit[:, :PATCH] + hit[:, PATCH:])
        picks = jnp.concatenate(picks, axis=0).astype(BF16)
        parts = [dot(picks, slave[k] if slot == 0 else rows[slot, k]) for k in range(4)]
        for d in range(NZ):
            packed[d, slot] = jnp.concatenate(
                [part[d * 8 : d * 8 + 8] for part in parts], axis=0
            ).astype(BF16)

    returns = {}

    def process(d):
        left = packed[d].reshape(256, NODE)
        out = dot(left, mortar[...] if d == 0 else table[d]).astype(BF16).reshape(8, 32, NODE)
        product[d] = out
        returned[d, 0] = out[0]
        for dx, dc in row_peers[1:]:
            slot, there = dx * 2 + dc, ((-dx) % NX) * 2 + dc
            returns[d, slot] = send(
                product.at[d, slot],
                returned.at[d, there],
                r_send.at[d, slot],
                r_recv.at[d, there],
                at(dx=dx, dc=dc),
            )

    lanes = iota((PATCH, 256), 1).astype(F32)

    def unpack(d, totals):
        for dx, dc in row_peers[1:]:
            returns[d, dx * 2 + dc].wait_recv()
        right = returned[d].reshape(256, NODE)
        result = []
        for k in range(4):
            total = totals[k] if totals is not None else None
            for j in range(2):
                choose = (lanes + (d * 256.0 - k * 8.0) == codes[j]).astype(F32).astype(BF16)
                term = weights[j] * dot(choose, right)
                total = term if total is None else total + term
            result.append(total)
        return result

    def unpack_into(d, first=False):
        totals = None if first else [blocks_out[k] for k in range(4)]
        for k, total in enumerate(unpack(d, totals)):
            blocks_out[k] = total

    pack(0)
    pass_tables(0, 0)
    s_copy["up0"].wait_recv()
    send_rows("far0", 6, pair(6, 0), pair(4, 0), at(dx=1))
    send_rows("up0s", 7, pair(6, 0), pair(7, 0), at(dc=1))
    s_copy["down1"].wait_recv()
    send_rows("far1", 8, pair(2, 1), pair(4, 1), at(dx=-1))
    send_rows("down1s", 9, pair(2, 1), pair(3, 1), at(dc=1))
    s_copy["side0"].wait_recv()
    s_copy["side1"].wait_recv()
    pack(1)
    pass_tables(0, 1)
    s_copy["up1"].wait_recv()
    send_rows("up1s", 10, pair(6, 1), pair(7, 1), at(dc=1))
    s_copy["down0"].wait_recv()
    send_rows("down0s", 11, pair(2, 0), pair(3, 0), at(dc=1))
    pack(6)
    pack(2)
    for key in ("up0s", "up1s"):
        s_copy[key].wait_recv()
    pack(7)
    for key in ("down0s", "down1s"):
        s_copy[key].wait_recv()
    pack(3)
    pass_tables(1, 0)
    s_copy["far0"].wait_recv()
    send_rows("far0s", 12, pair(4, 0), pair(5, 0), at(dc=1))
    s_copy["far1"].wait_recv()
    send_rows("far1s", 13, pair(4, 1), pair(5, 1), at(dc=1))
    pack(4)
    for key in ("far0s", "far1s"):
        s_copy[key].wait_recv()
    pack(5)
    process(0)
    process(7)
    process(1)
    pass_tables(1, 1)
    process(6)
    process(2)
    unpack_into(0, first=True)
    pass_tables(2, 0)
    unpack_into(7)
    unpack_into(1)

    flag = column(active[...].astype(F32))
    count = jnp.sum(active[...].astype(F32), axis=1, keepdims=True)
    local_row = corner_local[...]
    global_row = corner_global[...]
    patch_row, node_row = local_row // NODE, local_row % NODE
    patch_column = column(patch_row.astype(F32))
    node_column = column(node_row.astype(F32))
    global_column = column(global_row.astype(F32))
    at_patch = (iota((CORNERS, PATCH), 1).astype(F32) == patch_column).astype(F32)
    at_node = (iota((CORNERS, NODE), 1).astype(F32) == node_column).astype(F32)
    at_global = (iota((CORNERS, COARSE), 1).astype(F32) == global_column).astype(F32)
    back = (iota((PATCH, CORNERS), 0) == patch_row).astype(F32)
    load_inverse.wait()
    for c in range(CORNERS):
        inverse_rows[c : c + 1, :] = inverse[pl.ds(corner_global_s[c], 1), :]
    pieces = jnp.concatenate(split3(coupling[...]), axis=0)
    for copy in factor_copies:
        copy.wait_recv()
    own_factor.wait()

    pass_tables(2, 1)
    process(5)
    process(3)
    unpack_into(6)
    unpack_into(2)
    tables[0, 3, 0].wait_recv()
    tables[1, 3, 1].wait_recv()
    process(4)
    unpack_into(5)
    unpack_into(3)
    blocks = unpack(4, [blocks_out[k] for k in range(4)])
    for k in range(4):
        blocks_out[k] = blocks[k]

    magnitude = jnp.sqrt(1.0 + (blocks[1] ** 2 + blocks[2] ** 2 + blocks[3] ** 2))
    residual = flag * blocks[0] / magnitude + (1.0 - flag) * multiplier[...]
    rounded = residual.astype(BF16)
    halo[2] = rounded
    halo_copies = [
        send(halo.at[2], halo.at[0], h_send.at[0], h_recv.at[0], behind),
        send(halo.at[2], halo.at[1], h_send.at[1], h_recv.at[1], before),
    ]
    reduced[own_rows, :] = dot(rounded, factor[...]).astype(BF16)
    reduced_copies = [
        send(reduced.at[own_rows], reduced.at[own_rows], y_send.at[1, dy], y_recv.at[1, dy], at(dy=dy))
        for dy in range(1, NB)
    ]
    square = jnp.sum(jnp.sum(residual * residual, axis=0, keepdims=True), axis=1, keepdims=True)
    for copy in halo_copies:
        copy.wait_recv()
    left = jnp.where(sub > 0, halo[0].astype(F32), 0.0)
    right = jnp.where(sub < 63, halo[1].astype(F32), 0.0)
    for copy in reduced_copies:
        copy.wait_recv()
    applied = dot(pieces, reduced[...])
    applied = applied[0:PATCH] + (applied[PATCH : 2 * PATCH] + applied[2 * PATCH :])
    image = applied - 0.25 * (left + right)

    at_corner = jnp.dot(at_patch, image, precision=lax.Precision.HIGHEST, preferred_element_type=F32)
    values = jnp.sum(at_corner * at_node, axis=1, keepdims=True)
    lane = iota((1, 128), 1)
    extra = jnp.where(lane == 0, square, jnp.where(lane == 1, count, 0.0))
    sum_a[0] = jnp.concatenate([jnp.sum(values * at_global, axis=0, keepdims=True), extra], axis=1)
    copies = []
    for i, (dx, dy) in enumerate(group_a):
        if i:
            there = ((-dx) % NX) * NB + (-dy) % NB
            copies.append(
                send(sum_a.at[0], sum_a.at[there], a_send.at[i], a_recv.at[there], at(dx=dx, dy=dy))
            )
    for copy in copies:
        copy.wait_recv()
    total = sum_a[0]
    for i in range(1, 16):
        total = total + sum_a[i]
    sum_b[0] = total
    copies = []
    for i, (dz, dc) in enumerate(group_b):
        if i:
            there = ((-dz) % NZ) * 2 + dc
            copies.append(
                send(sum_b.at[0], sum_b.at[there], b_send.at[i], b_recv.at[there], at(dz=dz, dc=dc))
            )
    for copy in copies:
        copy.wait_recv()
    total = sum_b[0]
    for i in range(1, 16):
        total = total + sum_b[i]
    square_sum = total[:, COARSE : COARSE + 1]
    active_count = total[:, COARSE + 1 : COARSE + 2]
    scale = jnp.sqrt(active_count * float(NODE) / (square_sum + 1e-6))
    coarse = jnp.sum(inverse_rows[...] * total[:, :COARSE], axis=1, keepdims=True)
    correction = jnp.dot(
        back, coarse * at_node, precision=lax.Precision.HIGHEST, preferred_element_type=F32
    )
    image_out[...] = scale * (image + correction)
    for copy in sends:
        copy.wait_send()


def body(
    slave_blocks,
    masters,
    master_weight,
    active,
    multiplier,
    mortar,
    schur_rows,
    patch_coupling,
    corner_local,
    corner_global,
    coarse_inverse,
):
    vmem = pl.BlockSpec(memory_space=pltpu.VMEM)
    smem = pl.BlockSpec(memory_space=pltpu.SMEM)
    dma = pltpu.SemaphoreType.DMA
    blocks, image = pl.pallas_call(
        kernel,
        out_shape=(
            jax.ShapeDtypeStruct((4, PATCH, NODE), F32),
            jax.ShapeDtypeStruct((PATCH, NODE), F32),
        ),
        in_specs=[vmem] * 10 + [smem, pl.BlockSpec(memory_space=pl.ANY)],
        out_specs=(vmem, vmem),
        scratch_shapes=[
            pltpu.VMEM((NZ, NODE, NODE), BF16),
            pltpu.VMEM((8, 4, PATCH, NODE), BF16),
            pltpu.VMEM((8, 8, PATCH), I32),
            pltpu.VMEM((NZ, 8, 32, NODE), BF16),
            pltpu.VMEM((NZ, 8, 32, NODE), BF16),
            pltpu.VMEM((NZ, 8, 32, NODE), BF16),
            pltpu.VMEM((NODE, NODE), BF16),
            pltpu.VMEM((NODE, NODE), BF16),
            pltpu.VMEM((3, PATCH, NODE), BF16),
            pltpu.VMEM((16, 1, MESSAGE), F32),
            pltpu.VMEM((16, 1, MESSAGE), F32),
            pltpu.VMEM((COARSE, COARSE), F32),
            pltpu.VMEM((CORNERS, COARSE), F32),
            dma((2, 4, 2)),
            dma((2, 4, 2)),
            dma((14,)),
            dma((14,)),
            dma((8,)),
            dma((8,)),
            dma((8, 8)),
            dma((8, 8)),
            dma((2, 4)),
            dma((2, 4)),
            dma((2,)),
            dma((2,)),
            dma((16,)),
            dma((16,)),
            dma((16,)),
            dma((16,)),
            dma((2,)),
        ],
        compiler_params=pltpu.CompilerParams(
            collective_id=0, has_side_effects=True, vmem_limit_bytes=48 * 1024 * 1024
        ),
        name="newton_step",
    )(
        slave_blocks.transpose(1, 0, 2),
        masters.T,
        master_weight.T,
        active.reshape(1, PATCH),
        multiplier,
        mortar,
        schur_rows,
        patch_coupling,
        corner_local.reshape(1, CORNERS),
        corner_global.reshape(1, CORNERS),
        corner_global,
        coarse_inverse,
    )
    return blocks.transpose(1, 0, 2), image


def solution(mesh):
    split = P(("sub", "blk"))
    in_specs = (split,) * 10 + (P(),)
    return jax.shard_map(
        body, mesh=mesh, in_specs=in_specs, out_specs=(split, split), check_vma=False
    )
```

time: 329 us -> 92.3 us (0.28)
  blocking collectives: 239 us -> 0 us
  Pallas kernels: 0 us -> 80.7 us
  waiting for transfers between devices: 38.5 us -> 0 us
  local copies, waits for them, and re-layouts: 23.7 us -> 10.6 us
  starting transfers between devices: 10.3 us -> 0 us
  matrix products: 9.62 us -> 0 us
  other arithmetic: 5.43 us -> 0 us
    psum x2 -> x0, blocking collectives: 153 us -> none  [the longest x1 76.5 us: body(): total_sq, total_count = lax.psum((local_sq, local_count), ('sub', 'blk'))]
    pallas_call x0 -> x1, Pallas kernels: none -> 80.7 us  [body(): pl.pallas_call(kernel, out_shape=(jax.ShapeDtypeStruct((4, PATCH, NODE),...]
    all_to_all x1 -> x0, blocking collectives: 64.1 us -> none  [body(): lax.all_to_all(outgoing.reshape(subdomains, capacity, 4 * node_count), 's...]
    all_to_all x1 -> x0, waiting for transfers between devices: 38.5 us -> none  [body(): lax.all_to_all(product.reshape(arrived.shape), 'sub', split_axis=0, conca...]
    all_gather x2 -> x0, blocking collectives: 21.7 us -> none  [the longest x1 11.8 us: body(): lax.all_gather(schur_rows, 'blk', axis=0, tiled=True)]
    reshape x5 -> x0, local copies, waits for them, and re-layouts: 12.2 us -> none  [the longest x1 4.36 us: body(): product.reshape(arrived.shape)]
    dot_general x6 -> x0, matrix products: 9.62 us -> none  [the longest x1 5.64 us: body(): coarse = jnp.dot(coarse_inverse, assembled, precision=lax.Precision.HIGHEST)]
    unnamed x22 -> x21, local copies, waits for them, and re-layouts: 2.47 us -> 10.6 us
  transfers between devices with their start and end apart: 3 -> 0, of which waited for: 1 -> 0; matrix products, arithmetic and copies ran while one was open for 0% -> 0% of each run, Pallas kernels for 0% -> 0%
where the time goes in v1:
time: 92.3 us; the launch traced here: 92 us
  Pallas kernels  80.7 us (87%)
  local copies, waits for them, and re-layouts  10.6 us (11%)
    pallas_call x1, Pallas kernels, body(): pl.pallas_call(kernel, out_shape=(jax.ShapeDtypeStruct((4, PATCH, NODE),...  80.7 us
    unnamed x21, local copies, waits for them, and re-layouts  10.6 us

profile of v1, /device:TPU:1, one launch (start us, length us, event | category | flops | bytes accessed | tf_op | source)
XLA Modules:
  0.0 92.0 jit_solution(5406440793478516844)
XLA Ops:
  0.6 1.1 %copy.16 = bf16[128,4,512]{2,0,1:T(8,128)(2,1)S(1)} copy(bf16[128,4,512]{2,1,0:T(4,128)(2,1)} %param.11) | data formatting | bytes 1048576 | tf_op args[0]
  1.8 0.0 copy-start
  1.8 1.0 %copy-done = bf16[512,512]{1,0:T(8,128)(2,1)S(1)} copy-done((bf16[512,512]{1,0:T(8,128)(2,1)S(1)}, bf16[512,512]{1,0:T(8,128)(2,1)}, u32[]{:S(2)}) %copy-start) | copy-done | bytes 524312
  2.8 0.0 copy-start.1
  2.8 0.9 %copy-done.1 = f32[128,512]{1,0:T(8,128)S(1)} copy-done((f32[128,512]{1,0:T(8,128)S(1)}, f32[128,512]{1,0:T(8,128)}, u32[]{:S(2)}) %copy-start.1) | copy-done | bytes 262168
  3.8 0.0 copy-start.2
  3.8 0.9 %copy-done.2 = f32[128,512]{1,0:T(8,128)S(1)} copy-done((f32[128,512]{1,0:T(8,128)S(1)}, f32[128,512]{1,0:T(8,128)}, u32[]{:S(2)}) %copy-start.2) | copy-done | bytes 262168
  4.7 0.0 copy-start.3
  4.7 0.9 copy-done.3
  5.6 0.0 copy-start.4
  5.6 0.7 copy-done.4
  6.3 0.0 copy-start.5
  6.3 0.7 copy-done.5
  7.0 0.0 copy-start.6
  7.0 0.7 copy-done.6
  7.6 0.0 copy-start.7
  7.6 0.7 copy-done.7
  8.3 0.0 copy-start.8
  8.3 0.7 copy-done.8
  8.9 80.7 %newton_step.1 = (f32[4,128,512]{2,1,0:T(8,128)S(1)}, f32[128,512]{1,0:T(8,128)S(1)}) custom-call(bf16[4,128,512]{2,1,0:T(8,128)(2,1)S(1)} %bitcast.9, s32[2,128]{1,0:T(2,128)S(1)} %bitcast.12, f32[2,128]{1,0:T(2,128)S(1)} %bitcast.13, s32[1,128]{1,0:T(1,128)S(1)} %bitcast.14, f32[128,512]{1,0:T(8,128)S(1)} %copy-done.1, bf16[512,512]{1,0:T(8,128)(2,1)S(1)} %copy-done, ...), custom_call_target="tpu_custom_call" | custom-call | tf_op jit(solution)/shard_map/newton_step/pallas_call | solution.py:431
  89.7 1.6 %copy.14 = f32[128,4,512]{2,1,0:T(4,128)} copy(f32[128,4,512]{2,0,1:T(8,128)S(1)} %bitcast.10) | data formatting | bytes 2097152
  91.3 0.7 copy.18
Async XLA Ops:
  1.8 1.0 %copy-start = (bf16[512,512]{1,0:T(8,128)(2,1)S(1)}, bf16[512,512]{1,0:T(8,128)(2,1)}, u32[]{:S(2)}) copy-start(bf16[512,512]{1,0:T(8,128)(2,1)} %mortar.1) | copy-start | bytes 1572868
  2.8 0.9 %copy-start.1 = (f32[128,512]{1,0:T(8,128)S(1)}, f32[128,512]{1,0:T(8,128)}, u32[]{:S(2)}) copy-start(f32[128,512]{1,0:T(8,128)} %multiplier.1) | copy-start | bytes 786436
  3.8 0.9 %copy-start.2 = (f32[128,512]{1,0:T(8,128)S(1)}, f32[128,512]{1,0:T(8,128)}, u32[]{:S(2)}) copy-start(f32[128,512]{1,0:T(8,128)} %coupling.1) | copy-start | bytes 786436
  4.7 0.9 copy-start.3
  5.6 0.7 copy-start.4
  6.3 0.7 copy-start.5
  7.0 0.7 copy-start.6
  7.6 0.7 copy-start.7
  8.3 0.7 copy-start.8

commit v2 on v1

v2 whole, which is shorter than its diff:
```python
import functools

import jax
import jax.numpy as jnp
from jax import lax
from jax.experimental import pallas as pl
from jax.experimental.pallas import tpu as pltpu
from jax.sharding import PartitionSpec as P

NX, NZ, NB = 4, 8, 4
PATCH = 128
NODE = 512
CORNERS = 16
COARSE = 1024
MESSAGE = COARSE + 128
MESH = pl.DeviceIdType.MESH
F32, BF16, I32 = jnp.float32, jnp.bfloat16, jnp.int32


def iota(shape, dim):
    return lax.broadcasted_iota(I32, shape, dim)


def dot(a, b):
    return jnp.dot(a, b, preferred_element_type=F32)


def column(row):
    n = row.shape[1]
    return jnp.sum(jnp.where(iota((n, n), 0) == iota((n, n), 1), row, 0.0), axis=1, keepdims=True)


def split3(a):
    high = a.astype(BF16)
    rest = a - high.astype(F32)
    middle = rest.astype(BF16)
    low = (rest - middle.astype(F32)).astype(BF16)
    return high, middle, low


def kernel(
    slave_hbm,
    masters_hbm,
    weight_hbm,
    active_hbm,
    multiplier_hbm,
    mortar,
    schur_hbm,
    coupling_hbm,
    corner_local_hbm,
    corner_global_hbm,
    corner_global_s,
    coarse_inverse,
    blocks_out,
    image_out,
    slave,
    masters,
    weight,
    active,
    multiplier,
    schur,
    coupling,
    corner_local,
    corner_global,
    table,
    rows,
    names,
    packed,
    product,
    returned,
    factor,
    reduced,
    halo,
    sum_a,
    sum_b,
    inverse,
    inverse_rows,
    t_send,
    t_recv,
    s_send,
    s_recv,
    n_send,
    n_recv,
    r_send,
    r_recv,
    y_send,
    y_recv,
    h_send,
    h_recv,
    a_send,
    a_recv,
    b_send,
    b_recv,
    local_sem,
    slave_raw,
    pieces,
    corner_out,
    corner_in,
    halo_facts,
    at_node,
    at_global,
    halo_node,
    halo_patch,
):
    sub = lax.axis_index("sub")
    blk = lax.axis_index("blk")
    x = sub // (2 * NZ)
    z = (sub // 2) % NZ
    core = sub % 2

    def at(dx=0, dz=0, dc=0, dy=0):
        xx = (x + dx) % NX
        zz = (z + dz) % NZ
        return ((xx * NZ + zz) * 2 + (core + dc) % 2, (blk + dy) % NB)

    sends = []

    def send(src, dst, send_sem, recv_sem, to):
        copy = pltpu.make_async_remote_copy(
            src_ref=src,
            dst_ref=dst,
            send_sem=send_sem,
            recv_sem=recv_sem,
            device_id=to,
            device_id_type=MESH,
        )
        copy.start()
        sends.append(copy)
        return copy

    loads = {}
    for i, (name, src, dst) in enumerate(
        (
            ("masters", masters_hbm, masters),
            ("slave", slave_hbm, slave_raw),
            ("schur", schur_hbm, schur),
            ("weight", weight_hbm, weight),
            ("mortar", mortar, table.at[0]),
            ("active", active_hbm, active),
            ("local", corner_local_hbm, corner_local),
            ("global", corner_global_hbm, corner_global),
            ("multiplier", multiplier_hbm, multiplier),
            ("coupling", coupling_hbm, coupling),
        )
    ):
        loads[name] = pltpu.make_async_copy(src, dst, local_sem.at[i])
        loads[name].start()

    row_peers = [(dx, dc) for dx in range(NX) for dc in range(2)]
    group_a = [(dx, dy) for dx in range(NX) for dy in range(NB)]
    group_b = [(dz, dc) for dz in range(NZ) for dc in range(2)]
    greet = {(dx, 0, dc, 0) for dx, dc in row_peers}
    greet |= {(dx, 0, 0, dy) for dx, dy in group_a}
    greet |= {(0, dz, dc, 0) for dz, dc in group_b}
    greet = sorted(greet - {(0, 0, 0, 0)})
    before, behind = ((sub + 63) % 64, blk), ((sub + 1) % 64, blk)
    barrier = pltpu.get_barrier_semaphore()
    for dx, dz, dc, dy in greet:
        pl.semaphore_signal(barrier, inc=1, device_id=at(dx, dz, dc, dy), device_id_type=MESH)
    for neighbour in (before, behind):
        pl.semaphore_signal(barrier, inc=1, device_id=neighbour, device_id_type=MESH)
    loads["masters"].wait()
    names[0] = jnp.zeros((8, PATCH), I32)
    names[0, 0:2, :] = masters[...]
    pl.semaphore_wait(barrier, len(greet) + 2)

    orders = ((0, 2, 1, 3), (1, 3, 0, 2))
    tables = {}

    def chunk(ref, q):
        return ref.at[:, pl.ds(q * 128, 128)]

    def send_table(way, step, q):
        slot = (-step) % NZ if way == 0 else step
        land = (-step - 1) % NZ if way == 0 else step + 1
        src = mortar if step == 0 else table.at[slot]
        tables[way, step, q] = send(
            chunk(src, q),
            chunk(table.at[land], q),
            t_send.at[way, step, q],
            t_recv.at[way, step, q],
            at(dz=1 if way == 0 else -1),
        )

    def pass_tables(step, turns):
        for turn in turns:
            for way in (0, 1):
                q = orders[way][turn]
                tables[way, step, q].wait_recv()
                if step < 2 or (step == 2 and turn < 2):
                    send_table(way, step + 1, q)

    for turn in range(4):
        for way in (0, 1):
            send_table(way, 0, orders[way][turn])

    names_copies = [
        send(
            names.at[0],
            names.at[((-dx) % NX) * 2 + dc],
            n_send.at[dx * 2 + dc],
            n_recv.at[((-dx) % NX) * 2 + dc],
            at(dx=dx, dc=dc),
        )
        for dx, dc in row_peers[1:]
    ]

    def pair(slot, h):
        return rows.at[slot, pl.ds(2 * h, 2)]

    loads["slave"].wait()
    for k in range(4):
        slave[k] = slave_raw[:, k, :]
    own = [slave.at[pl.ds(0, 2)], slave.at[pl.ds(2, 2)]]
    s_copy = {}

    def send_rows(key, number, src, dst, to):
        s_copy[key] = send(src, dst, s_send.at[number], s_recv.at[number], to)

    send_rows("up0", 0, own[0], pair(6, 0), at(dx=1))
    send_rows("down1", 1, own[1], pair(2, 1), at(dx=-1))
    send_rows("up1", 2, own[1], pair(6, 1), at(dx=1))
    send_rows("down0", 3, own[0], pair(2, 0), at(dx=-1))
    send_rows("side0", 4, own[0], pair(1, 0), at(dc=1))
    send_rows("side1", 5, own[1], pair(1, 1), at(dc=1))

    loads["schur"].wait()
    factor_copies = []
    own_rows = pl.ds(pl.multiple_of(blk * PATCH, PATCH), PATCH)
    for dy in range(1, NB):
        factor_copies.append(
            send(schur, factor.at[own_rows], y_send.at[0, dy], y_recv.at[0, dy], at(dy=dy))
        )
    loads["inverse"] = pltpu.make_async_copy(coarse_inverse, inverse, local_sem.at[10])
    loads["inverse"].start()
    own_factor = pltpu.make_async_copy(schur, factor.at[own_rows], local_sem.at[11])
    own_factor.start()

    for name in ("local", "global", "coupling"):
        loads[name].wait()
    local_row, global_row = corner_local[...], corner_global[...]
    patch_row, node_row = local_row // NODE, local_row % NODE
    at_patch = (iota((CORNERS, PATCH), 1).astype(F32) == column(patch_row.astype(F32))).astype(F32).astype(BF16)
    corner_rows = 0.0
    for i, piece in enumerate(split3(coupling[...])):
        pieces[i * PATCH : (i + 1) * PATCH] = piece
        corner_rows = corner_rows + dot(at_patch, piece)
    padding = jnp.zeros((1, 128 - CORNERS), F32)
    facts = [jnp.concatenate([r.astype(F32), padding], axis=1) for r in (node_row, global_row, patch_row)]
    facts = jnp.concatenate(facts + [jnp.zeros((5, 128), F32)], axis=0)
    for i in range(NB):
        corner_out[i] = jnp.concatenate([corner_rows[:, i * 128 : (i + 1) * 128], facts], axis=0)
    corner_in[0] = corner_out[blk]
    corner_copies = [
        send(
            corner_out.at[(blk + dy) % NB],
            corner_in.at[(-dy) % NB],
            y_send.at[2, dy],
            y_recv.at[2, dy],
            at(dy=dy),
        )
        for dy in range(1, NB)
    ]
    facts_ref = corner_out.at[0, pl.ds(CORNERS, 8)]
    corner_copies += [
        send(facts_ref, halo_facts.at[0], h_send.at[2], h_recv.at[2], behind),
        send(facts_ref, halo_facts.at[1], h_send.at[3], h_recv.at[3], before),
    ]

    strict = (iota((256, 256), 0) < iota((256, 256), 1)).astype(F32).astype(BF16)

    def entries(name):
        return jnp.concatenate([name[0:1, :], name[1:2, :]], axis=1)

    own_entries = entries(masters[...])
    named = (own_entries == iota((64, 256), 0)).astype(F32)
    rank = jnp.sum(named * dot(named.astype(BF16), strict), axis=0, keepdims=True)
    ez, ex, ec = (own_entries // 2) % NZ, own_entries // (2 * NZ), own_entries % 2
    place = ((ez - z + NZ) % NZ) * 256 + (((ex - x + NX) % NX) * 2 + (ec + core) % 2) * 32
    place = place.astype(F32) + rank
    codes = [column(place[:, j * PATCH : (j + 1) * PATCH]) for j in range(2)]
    loads["weight"].wait()
    weights = [column(weight[j : j + 1, :]) for j in range(2)]

    for copy in names_copies:
        copy.wait_recv()
    mine = ((x * NZ + (z + iota((8, 256), 0)) % NZ) * 2 + core).astype(I32)
    named = jnp.concatenate(
        [(entries(names[slot]) == mine).astype(F32) for slot in range(8)], axis=0
    )
    ranks = jnp.where(named > 0.0, dot(named.astype(BF16), strict), -1.0)
    wanted = iota((8, 256), 0).astype(F32)

    def pack(slot):
        picks = []
        for d in range(NZ):
            line = ranks[slot * 8 + d : slot * 8 + d + 1, :]
            hit = (line == wanted).astype(F32)
            picks.append(hit[:, :PATCH] + hit[:, PATCH:])
        picks = jnp.concatenate(picks, axis=0).astype(BF16)
        parts = [dot(picks, slave[k] if slot == 0 else rows[slot, k]) for k in range(4)]
        for d in range(NZ):
            packed[d, slot] = jnp.concatenate(
                [part[d * 8 : d * 8 + 8] for part in parts], axis=0
            ).astype(BF16)

    returns = {}

    def process(d, part=None):
        width = NODE if part is None else 256
        cols = pl.ds(0 if part is None else part * 256, width)
        sem = d if part != 1 else NZ
        out = dot(packed[d].reshape(256, NODE), table[d, :, cols]).astype(BF16)
        out = out.reshape(8, 32, width)
        product[d, :, :, cols] = out
        returned[d, 0, :, cols] = out[0]
        for dx, dc in row_peers[1:]:
            slot, there = dx * 2 + dc, ((-dx) % NX) * 2 + dc
            returns[sem, slot] = send(
                product.at[d, slot, :, cols],
                returned.at[d, there, :, cols],
                r_send.at[sem, slot],
                r_recv.at[sem, there],
                at(dx=dx, dc=dc),
            )

    lanes = iota((PATCH, 256), 1).astype(F32)

    def unpack(d, part=None, first=False):
        width = NODE if part is None else 256
        cols = pl.ds(0 if part is None else part * 256, width)
        sem = d if part != 1 else NZ
        for dx, dc in row_peers[1:]:
            returns[sem, dx * 2 + dc].wait_recv()
        right = returned[d, :, :, cols].reshape(256, width)
        for k in range(4):
            total = None if first else blocks_out[k, :, cols]
            for j in range(2):
                choose = (lanes + (d * 256.0 - k * 8.0) == codes[j]).astype(F32).astype(BF16)
                term = weights[j] * dot(choose, right)
                total = term if total is None else total + term
            blocks_out[k, :, cols] = total

    pack(0)
    s_copy["side0"].wait_recv()
    s_copy["side1"].wait_recv()
    pack(1)
    pass_tables(0, (0,))
    s_copy["up0"].wait_recv()
    send_rows("far0", 6, pair(6, 0), pair(4, 0), at(dx=1))
    send_rows("up0s", 7, pair(6, 0), pair(7, 0), at(dc=1))
    s_copy["down1"].wait_recv()
    send_rows("far1", 8, pair(2, 1), pair(4, 1), at(dx=-1))
    send_rows("down1s", 9, pair(2, 1), pair(3, 1), at(dc=1))
    pass_tables(0, (1, 2))
    s_copy["up1"].wait_recv()
    send_rows("up1s", 10, pair(6, 1), pair(7, 1), at(dc=1))
    s_copy["down0"].wait_recv()
    send_rows("down0s", 11, pair(2, 0), pair(3, 0), at(dc=1))
    pass_tables(0, (3,))
    pack(6)
    pack(2)
    pass_tables(1, (0,))
    for key in ("up0s", "up1s"):
        s_copy[key].wait_recv()
    pack(7)
    for key in ("down0s", "down1s"):
        s_copy[key].wait_recv()
    pack(3)
    pass_tables(1, (1,))
    s_copy["far0"].wait_recv()
    send_rows("far0s", 12, pair(4, 0), pair(5, 0), at(dc=1))
    s_copy["far1"].wait_recv()
    send_rows("far1s", 13, pair(4, 1), pair(5, 1), at(dc=1))
    pack(4)
    for key in ("far0s", "far1s"):
        s_copy[key].wait_recv()
    pack(5)
    process(7)
    process(1)
    pass_tables(1, (2, 3))
    process(6)
    process(2)
    loads["mortar"].wait()
    process(0)
    pass_tables(2, (0,))
    unpack(7, first=True)
    pass_tables(2, (1,))
    unpack(1)

    loads["active"].wait()
    loads["multiplier"].wait()
    flag = column(active[...].astype(F32))
    count = jnp.sum(active[...].astype(F32), axis=1, keepdims=True)
    loads["inverse"].wait()
    for c in range(CORNERS):
        inverse_rows[c : c + 1, :] = inverse[pl.ds(corner_global_s[c], 1), :]
    for copy in corner_copies:
        copy.wait_recv()
    own_nodes = None
    for i in range(NB + 2):
        facts = corner_in[i, CORNERS : CORNERS + 8, :] if i < NB else halo_facts[i - NB]
        nodes = (iota((CORNERS, NODE), 1).astype(F32) == column(facts[0:1, :CORNERS])).astype(F32)
        span = slice(i * CORNERS, (i + 1) * CORNERS)
        if i == 0:
            own_nodes = nodes
        if i < NB:
            at_node[span] = nodes.astype(BF16)
        else:
            quarter = jnp.where(sub > 0 if i == NB else sub < 63, -0.25, 0.0)
            there = slice((i - NB) * CORNERS, (i - NB + 1) * CORNERS)
            halo_node[there] = nodes * quarter
            halo_patch[there] = (
                (iota((CORNERS, PATCH), 1).astype(F32) == column(facts[2:3, :CORNERS])).astype(F32).astype(BF16)
            )
        at_global[span] = (
            iota((CORNERS, COARSE), 1).astype(F32) == column(facts[1:2, :CORNERS])
        ).astype(F32)
    patch_row3 = jnp.concatenate([patch_row] * 3, axis=1)
    back = (iota((PATCH, 3 * CORNERS), 0) == patch_row3).astype(F32).astype(BF16)
    for copy in factor_copies:
        copy.wait_recv()
    own_factor.wait()

    pass_tables(2, (2, 3))
    process(5)
    process(3)
    unpack(6)
    unpack(2)
    pass_tables(3, (0,))
    process(4, 0)
    unpack(0)
    unpack(5)
    pass_tables(3, (1,))
    process(4, 1)
    unpack(3)
    unpack(4, 0)
    unpack(4, 1)
    blocks = [blocks_out[k] for k in range(4)]

    magnitude = jnp.sqrt(1.0 + (blocks[1] ** 2 + blocks[2] ** 2 + blocks[3] ** 2))
    residual = flag * blocks[0] / magnitude + (1.0 - flag) * multiplier[...]
    rounded = residual.astype(BF16)
    halo[2] = rounded
    own_reduced = dot(rounded, factor[...]).astype(BF16)
    reduced[own_rows, :] = own_reduced

    picked = lax.dot_general(
        at_node[...], own_reduced, (((1,), (1,)), ((), ())), preferred_element_type=F32
    )
    values = jnp.sum(picked * corner_in[:, 0:CORNERS, :].reshape(64, PATCH), axis=1, keepdims=True)
    beside = jnp.sum(dot(halo_patch[...], rounded) * halo_node[...], axis=1, keepdims=True)
    values = jnp.concatenate([values, beside], axis=0)
    square = jnp.sum(jnp.sum(residual * residual, axis=0, keepdims=True), axis=1, keepdims=True)
    lane = iota((1, 128), 1)
    extra = jnp.where(lane == 0, square, jnp.where(lane == 1, count, 0.0))
    sum_a[0] = jnp.concatenate(
        [jnp.sum(values * at_global[...], axis=0, keepdims=True), extra], axis=1
    )

    def hops(step, around):
        return min(step, around - step)

    def exchange(buffer, send_sem, recv_sem, group):
        copies = []
        for i, distance, there, to in sorted(group, key=lambda g: -g[1]):
            copies.append(
                send(buffer.at[0], buffer.at[there], send_sem.at[i], recv_sem.at[there], at(**to))
            )
        return copies

    def gather(buffer, copies):
        for copy in copies:
            copy.wait_recv()
        total = buffer[0]
        for i in range(1, 16):
            total = total + buffer[i]
        return total

    copies = exchange(
        sum_a,
        a_send,
        a_recv,
        [
            (
                dx * NB + dy,
                hops(dx, NX) + hops(dy, NB),
                ((-dx) % NX) * NB + (-dy) % NB,
                dict(dx=dx, dy=dy),
            )
            for dx, dy in group_a[1:]
        ],
    )
    reduced_copies = [
        send(reduced.at[own_rows], reduced.at[own_rows], y_send.at[1, dy], y_recv.at[1, dy], at(dy=dy))
        for dy in (2, 1, 3)
    ]
    halo_copies = [
        send(halo.at[2], halo.at[0], h_send.at[0], h_recv.at[0], behind),
        send(halo.at[2], halo.at[1], h_send.at[1], h_recv.at[1], before),
    ]
    sum_b[0] = gather(sum_a, copies)
    copies = exchange(
        sum_b,
        b_send,
        b_recv,
        [
            (dz * 2 + dc, hops(dz, NZ) + 0.5 * dc, ((-dz) % NZ) * 2 + dc, dict(dz=dz, dc=dc))
            for dz, dc in group_b[1:]
        ],
    )
    for copy in reduced_copies + halo_copies:
        copy.wait_recv()
    left = jnp.where(sub > 0, halo[0].astype(F32), 0.0)
    right = jnp.where(sub < 63, halo[1].astype(F32), 0.0)
    applied = dot(pieces[...], reduced[...])
    applied = applied[0:PATCH] + (applied[PATCH : 2 * PATCH] + applied[2 * PATCH :])
    image_out[...] = applied - 0.25 * (left + right)
    total = gather(sum_b, copies)
    square_sum = total[:, COARSE : COARSE + 1]
    active_count = total[:, COARSE + 1 : COARSE + 2]
    scale = jnp.sqrt(active_count * float(NODE) / (square_sum + 1e-6))
    coarse = jnp.sum(inverse_rows[...] * total[:, :COARSE], axis=1, keepdims=True)
    correction = dot(back, jnp.concatenate(split3(coarse * own_nodes), axis=0))
    image_out[...] = scale * (image_out[...] + correction)
    for copy in sends:
        copy.wait_send()


def body(
    slave_blocks,
    masters,
    master_weight,
    active,
    multiplier,
    mortar,
    schur_rows,
    patch_coupling,
    corner_local,
    corner_global,
    coarse_inverse,
):
    vmem = pl.BlockSpec(memory_space=pltpu.VMEM)
    hbm = pl.BlockSpec(memory_space=pltpu.HBM)
    smem = pl.BlockSpec(memory_space=pltpu.SMEM)
    dma = pltpu.SemaphoreType.DMA
    blocks, image = pl.pallas_call(
        kernel,
        out_shape=(
            jax.ShapeDtypeStruct((4, PATCH, NODE), F32),
            jax.ShapeDtypeStruct((PATCH, NODE), F32),
        ),
        in_specs=[hbm] * 10 + [smem, hbm],
        out_specs=(vmem, vmem),
        scratch_shapes=[
            pltpu.VMEM((4, PATCH, NODE), BF16),
            pltpu.VMEM((2, PATCH), I32),
            pltpu.VMEM((2, PATCH), F32),
            pltpu.VMEM((1, PATCH), I32),
            pltpu.VMEM((PATCH, NODE), F32),
            pltpu.VMEM((PATCH, NODE), BF16),
            pltpu.VMEM((PATCH, NODE), F32),
            pltpu.VMEM((1, CORNERS), I32),
            pltpu.VMEM((1, CORNERS), I32),
            pltpu.VMEM((NZ, NODE, NODE), BF16),
            pltpu.VMEM((8, 4, PATCH, NODE), BF16),
            pltpu.VMEM((8, 8, PATCH), I32),
            pltpu.VMEM((NZ, 8, 32, NODE), BF16),
            pltpu.VMEM((NZ, 8, 32, NODE), BF16),
            pltpu.VMEM((NZ, 8, 32, NODE), BF16),
            pltpu.VMEM((NODE, NODE), BF16),
            pltpu.VMEM((NODE, NODE), BF16),
            pltpu.VMEM((3, PATCH, NODE), BF16),
            pltpu.VMEM((16, 1, MESSAGE), F32),
            pltpu.VMEM((16, 1, MESSAGE), F32),
            pltpu.VMEM((COARSE, COARSE), F32),
            pltpu.VMEM((CORNERS, COARSE), F32),
            dma((2, 4, 4)),
            dma((2, 4, 4)),
            dma((14,)),
            dma((14,)),
            dma((8,)),
            dma((8,)),
            dma((9, 8)),
            dma((9, 8)),
            dma((3, 4)),
            dma((3, 4)),
            dma((4,)),
            dma((4,)),
            dma((16,)),
            dma((16,)),
            dma((16,)),
            dma((16,)),
            dma((12,)),
            pltpu.VMEM((PATCH, 4, NODE), BF16),
            pltpu.VMEM((3 * PATCH, NODE), BF16),
            pltpu.VMEM((NB, 24, 128), F32),
            pltpu.VMEM((NB, 24, 128), F32),
            pltpu.VMEM((2, 8, 128), F32),
            pltpu.VMEM((NB * CORNERS, NODE), BF16),
            pltpu.VMEM(((NB + 2) * CORNERS, COARSE), F32),
            pltpu.VMEM((2 * CORNERS, NODE), F32),
            pltpu.VMEM((2 * CORNERS, PATCH), BF16),
        ],
        compiler_params=pltpu.CompilerParams(
            collective_id=0, has_side_effects=True, vmem_limit_bytes=48 * 1024 * 1024
        ),
        name="newton_step",
    )(
        *[
            pltpu.with_memory_space_constraint(a, pltpu.HBM)
            for a in (
                slave_blocks,
                masters.T,
                master_weight.T,
                active.reshape(1, PATCH),
                multiplier,
                mortar,
                schur_rows,
                patch_coupling,
                corner_local.reshape(1, CORNERS),
                corner_global.reshape(1, CORNERS),
            )
        ],
        corner_global,
        pltpu.with_memory_space_constraint(coarse_inverse, pltpu.HBM),
    )
    return blocks.transpose(1, 0, 2), image


def solution(mesh):
    split = P(("sub", "blk"))
    in_specs = (split,) * 10 + (P(),)
    return jax.shard_map(
        body, mesh=mesh, in_specs=in_specs, out_specs=(split, split), check_vma=False
    )
```

time: 92.3 us -> 77.5 us (0.84)
  local copies, waits for them, and re-layouts: 10.6 us -> 2.35 us
  Pallas kernels: 80.7 us -> 74.4 us
    unnamed x21 -> x2, local copies, waits for them, and re-layouts: 10.6 us -> 2.35 us
    pallas_call x1, Pallas kernels: 80.7 us -> 74.4 us  [body(): pl.pallas_call(kernel, out_shape=(jax.ShapeDtypeStruct((4, PATCH, NODE),...]
where the time goes in v2:
time: 77.5 us; the launch traced here: 77.4 us
  Pallas kernels  74.4 us (96%)
  local copies, waits for them, and re-layouts  2.35 us (3%)
    pallas_call x1, Pallas kernels, body(): pl.pallas_call(kernel, out_shape=(jax.ShapeDtypeStruct((4, PATCH, NODE),...  74.4 us
    unnamed x2, local copies, waits for them, and re-layouts  2.35 us

profile of v2, /device:TPU:1, one launch (start us, length us, event | category | flops | bytes accessed | tf_op | source)
XLA Modules:
  0.0 77.4 jit_solution(2037652732866208078)
XLA Ops:
  0.6 74.4 %newton_step.1 = (f32[4,128,512]{2,1,0:T(8,128)S(1)}, f32[128,512]{1,0:T(8,128)S(1)}) custom-call(bf16[128,4,512]{2,1,0:T(4,128)(2,1)} %slave_hbm.1, s32[2,128]{1,0:T(2,128)} %bitcast.8, f32[2,128]{1,0:T(2,128)} %bitcast.9, s32[1,128]{1,0:T(1,128)} %bitcast.10, f32[128,512]{1,0:T(8,128)} %multiplier_hbm.1, bf16[512,512]{1,0:T(8,128)(2,1)} %mortar.1, ...), custom_call_target="tpu_custom_call" | custom-call | tf_op jit(solution)/shard_map/newton_step/pallas_call | solution.py:547
  75.0 1.6 %copy.13 = f32[128,4,512]{2,1,0:T(4,128)} copy(f32[128,4,512]{2,0,1:T(8,128)S(1)} %bitcast.6) | data formatting | bytes 2097152
  76.7 0.7 copy.15

commit v3 on v2

--- a/solution.py
+++ b/solution.py
@@ -15,6 +15,10 @@
 MESSAGE = COARSE + 128
 MESH = pl.DeviceIdType.MESH
 F32, BF16, I32 = jnp.float32, jnp.bfloat16, jnp.int32
+
+
+def slot_of(dx, dc):
+    return (0, 1, 3, 2)[dx % NX] * 2 + dc
 
 
 def iota(shape, dim):
@@ -49,7 +53,7 @@
     coupling_hbm,
     corner_local_hbm,
     corner_global_hbm,
-    corner_global_s,
+    corner_global_hbm1,
     coarse_inverse,
     blocks_out,
     image_out,
@@ -101,6 +105,8 @@
     at_global,
     halo_node,
     halo_patch,
+    corner_global_s,
+    blocks,
 ):
     sub = lax.axis_index("sub")
     blk = lax.axis_index("blk")
@@ -112,8 +118,6 @@
         xx = (x + dx) % NX
         zz = (z + dz) % NZ
         return ((xx * NZ + zz) * 2 + (core + dc) % 2, (blk + dy) % NB)
-
-    sends = []
 
     def send(src, dst, send_sem, recv_sem, to):
         copy = pltpu.make_async_remote_copy(
@@ -125,13 +129,16 @@
             device_id_type=MESH,
         )
         copy.start()
-        sends.append(copy)
         return copy
+
+    def await_bytes(ref, sem):
+        pltpu.make_async_copy(ref, ref, sem).wait()
 
     loads = {}
     for i, (name, src, dst) in enumerate(
         (
             ("masters", masters_hbm, masters),
+            ("scalars", corner_global_hbm1, corner_global_s),
             ("slave", slave_hbm, slave_raw),
             ("schur", schur_hbm, schur),
             ("weight", weight_hbm, weight),
@@ -151,7 +158,7 @@
     group_b = [(dz, dc) for dz in range(NZ) for dc in range(2)]
     greet = {(dx, 0, dc, 0) for dx, dc in row_peers}
     greet |= {(dx, 0, 0, dy) for dx, dy in group_a}
-    greet |= {(0, dz, dc, 0) for dz, dc in group_b}
+    greet |= {(0, dz, 0, 0) for dz in (1, NZ - 1)}
     greet = sorted(greet - {(0, 0, 0, 0)})
     before, behind = ((sub + 63) % 64, blk), ((sub + 1) % 64, blk)
     barrier = pltpu.get_barrier_semaphore()
@@ -177,7 +184,7 @@
         tables[way, step, q] = send(
             chunk(src, q),
             chunk(table.at[land], q),
-            t_send.at[way, step, q],
+            t_send.at[0],
             t_recv.at[way, step, q],
             at(dz=1 if way == 0 else -1),
         )
@@ -194,16 +201,10 @@
         for way in (0, 1):
             send_table(way, 0, orders[way][turn])
 
-    names_copies = [
+    for dx, dc in row_peers[1:]:
         send(
-            names.at[0],
-            names.at[((-dx) % NX) * 2 + dc],
-            n_send.at[dx * 2 + dc],
-            n_recv.at[((-dx) % NX) * 2 + dc],
-            at(dx=dx, dc=dc),
+            names.at[0], names.at[slot_of(-dx, dc)], n_send.at[0], n_recv.at[0], at(dx=dx, dc=dc)
         )
-        for dx, dc in row_peers[1:]
-    ]
 
     def pair(slot, h):
         return rows.at[slot, pl.ds(2 * h, 2)]
@@ -215,25 +216,21 @@
     s_copy = {}
 
     def send_rows(key, number, src, dst, to):
-        s_copy[key] = send(src, dst, s_send.at[number], s_recv.at[number], to)
-
-    send_rows("up0", 0, own[0], pair(6, 0), at(dx=1))
+        s_copy[key] = send(src, dst, s_send.at[0], s_recv.at[number], to)
+
+    send_rows("up0", 0, own[0], pair(4, 0), at(dx=1))
     send_rows("down1", 1, own[1], pair(2, 1), at(dx=-1))
-    send_rows("up1", 2, own[1], pair(6, 1), at(dx=1))
+    send_rows("up1", 2, own[1], pair(4, 1), at(dx=1))
     send_rows("down0", 3, own[0], pair(2, 0), at(dx=-1))
-    send_rows("side0", 4, own[0], pair(1, 0), at(dc=1))
-    send_rows("side1", 5, own[1], pair(1, 1), at(dc=1))
+    send_rows("side", 4, slave, rows.at[1], at(dc=1))
 
     loads["schur"].wait()
-    factor_copies = []
     own_rows = pl.ds(pl.multiple_of(blk * PATCH, PATCH), PATCH)
     for dy in range(1, NB):
-        factor_copies.append(
-            send(schur, factor.at[own_rows], y_send.at[0, dy], y_recv.at[0, dy], at(dy=dy))
-        )
-    loads["inverse"] = pltpu.make_async_copy(coarse_inverse, inverse, local_sem.at[10])
+        send(schur, factor.at[own_rows], y_send.at[0], y_recv.at[0], at(dy=dy))
+    loads["inverse"] = pltpu.make_async_copy(coarse_inverse, inverse, local_sem.at[11])
     loads["inverse"].start()
-    own_factor = pltpu.make_async_copy(schur, factor.at[own_rows], local_sem.at[11])
+    own_factor = pltpu.make_async_copy(schur, factor.at[own_rows], local_sem.at[12])
     own_factor.start()
 
     for name in ("local", "global", "coupling"):
@@ -251,21 +248,17 @@
     for i in range(NB):
         corner_out[i] = jnp.concatenate([corner_rows[:, i * 128 : (i + 1) * 128], facts], axis=0)
     corner_in[0] = corner_out[blk]
-    corner_copies = [
+    for dy in range(1, NB):
         send(
             corner_out.at[(blk + dy) % NB],
             corner_in.at[(-dy) % NB],
-            y_send.at[2, dy],
-            y_recv.at[2, dy],
+            y_send.at[2],
+            y_recv.at[2],
             at(dy=dy),
         )
-        for dy in range(1, NB)
-    ]
     facts_ref = corner_out.at[0, pl.ds(CORNERS, 8)]
-    corner_copies += [
-        send(facts_ref, halo_facts.at[0], h_send.at[2], h_recv.at[2], behind),
-        send(facts_ref, halo_facts.at[1], h_send.at[3], h_recv.at[3], before),
-    ]
+    send(facts_ref, halo_facts.at[0], h_send.at[1], h_recv.at[1], behind)
+    send(facts_ref, halo_facts.at[1], h_send.at[1], h_recv.at[1], before)
 
     strict = (iota((256, 256), 0) < iota((256, 256), 1)).astype(F32).astype(BF16)
 
@@ -276,14 +269,15 @@
     named = (own_entries == iota((64, 256), 0)).astype(F32)
     rank = jnp.sum(named * dot(named.astype(BF16), strict), axis=0, keepdims=True)
     ez, ex, ec = (own_entries // 2) % NZ, own_entries // (2 * NZ), own_entries % 2
-    place = ((ez - z + NZ) % NZ) * 256 + (((ex - x + NX) % NX) * 2 + (ec + core) % 2) * 32
+    away = (ex - x + NX) % NX
+    away = jnp.where(away == 2, 3, jnp.where(away == 3, 2, away))
+    place = ((ez - z + NZ) % NZ) * 256 + (away * 2 + (ec + core) % 2) * 32
     place = place.astype(F32) + rank
     codes = [column(place[:, j * PATCH : (j + 1) * PATCH]) for j in range(2)]
     loads["weight"].wait()
     weights = [column(weight[j : j + 1, :]) for j in range(2)]
 
-    for copy in names_copies:
-        copy.wait_recv()
+    await_bytes(names.at[pl.ds(1, 7)], n_recv.at[0])
     mine = ((x * NZ + (z + iota((8, 256), 0)) % NZ) * 2 + core).astype(I32)
     named = jnp.concatenate(
         [(entries(names[slot]) == mine).astype(F32) for slot in range(8)], axis=0
@@ -304,99 +298,98 @@
                 [part[d * 8 : d * 8 + 8] for part in parts], axis=0
             ).astype(BF16)
 
-    returns = {}
-
-    def process(d, part=None):
-        width = NODE if part is None else 256
-        cols = pl.ds(0 if part is None else part * 256, width)
-        sem = d if part != 1 else NZ
-        out = dot(packed[d].reshape(256, NODE), table[d, :, cols]).astype(BF16)
-        out = out.reshape(8, 32, width)
-        product[d, :, :, cols] = out
-        returned[d, 0, :, cols] = out[0]
+    near, far, everyone = (0, 6), (6, 8), (0, 8)
+
+    def process(d, group=everyone, lo=0, width=NODE, part=None):
+        first, last = group
+        cols = pl.ds(lo, width)
+        left = packed[d, first:last].reshape((last - first) * 32, NODE)
+        out = dot(left, table[d, :, cols]).astype(BF16).reshape(last - first, 32, width)
+        product[d, first:last, :, cols] = out
+        if first == 0:
+            returned[d, 0, :, cols] = out[0]
         for dx, dc in row_peers[1:]:
-            slot, there = dx * 2 + dc, ((-dx) % NX) * 2 + dc
-            returns[sem, slot] = send(
-                product.at[d, slot, :, cols],
-                returned.at[d, there, :, cols],
-                r_send.at[sem, slot],
-                r_recv.at[sem, there],
-                at(dx=dx, dc=dc),
-            )
+            if first <= slot_of(dx, dc) < last:
+                send(
+                    product.at[d, slot_of(dx, dc), :, cols],
+                    returned.at[d, slot_of(-dx, dc), :, cols],
+                    r_send.at[0],
+                    r_recv.at[NZ if part == 1 else d],
+                    at(dx=dx, dc=dc),
+                )
 
     lanes = iota((PATCH, 256), 1).astype(F32)
 
     def unpack(d, part=None, first=False):
         width = NODE if part is None else 256
         cols = pl.ds(0 if part is None else part * 256, width)
-        sem = d if part != 1 else NZ
-        for dx, dc in row_peers[1:]:
-            returns[sem, dx * 2 + dc].wait_recv()
+        await_bytes(returned.at[d, pl.ds(1, 7), :, cols], r_recv.at[NZ if part == 1 else d])
         right = returned[d, :, :, cols].reshape(256, width)
         for k in range(4):
-            total = None if first else blocks_out[k, :, cols]
+            total = None if first else blocks[k, :, cols]
             for j in range(2):
                 choose = (lanes + (d * 256.0 - k * 8.0) == codes[j]).astype(F32).astype(BF16)
                 term = weights[j] * dot(choose, right)
                 total = term if total is None else total + term
-            blocks_out[k, :, cols] = total
+            blocks[k, :, cols] = total
 
     pack(0)
-    s_copy["side0"].wait_recv()
-    s_copy["side1"].wait_recv()
+    s_copy["side"].wait_recv()
     pack(1)
     pass_tables(0, (0,))
     s_copy["up0"].wait_recv()
-    send_rows("far0", 6, pair(6, 0), pair(4, 0), at(dx=1))
-    send_rows("up0s", 7, pair(6, 0), pair(7, 0), at(dc=1))
+    send_rows("far0", 5, pair(4, 0), pair(6, 0), at(dx=1))
+    send_rows("up0s", 6, pair(4, 0), pair(5, 0), at(dc=1))
     s_copy["down1"].wait_recv()
-    send_rows("far1", 8, pair(2, 1), pair(4, 1), at(dx=-1))
-    send_rows("down1s", 9, pair(2, 1), pair(3, 1), at(dc=1))
+    send_rows("far1", 7, pair(2, 1), pair(6, 1), at(dx=-1))
+    send_rows("down1s", 8, pair(2, 1), pair(3, 1), at(dc=1))
     pass_tables(0, (1, 2))
     s_copy["up1"].wait_recv()
-    send_rows("up1s", 10, pair(6, 1), pair(7, 1), at(dc=1))
+    send_rows("up1s", 9, pair(4, 1), pair(5, 1), at(dc=1))
     s_copy["down0"].wait_recv()
-    send_rows("down0s", 11, pair(2, 0), pair(3, 0), at(dc=1))
+    send_rows("down0s", 10, pair(2, 0), pair(3, 0), at(dc=1))
     pass_tables(0, (3,))
-    pack(6)
+    pack(4)
     pack(2)
-    pass_tables(1, (0,))
     for key in ("up0s", "up1s"):
         s_copy[key].wait_recv()
-    pack(7)
+    pack(5)
     for key in ("down0s", "down1s"):
         s_copy[key].wait_recv()
     pack(3)
+    loads["mortar"].wait()
+    process(0, near)
+    pass_tables(1, (0,))
+    process(7, near)
+    process(1, near)
+    s_copy["far0"].wait_recv()
+    send_rows("far0s", 11, pair(6, 0), pair(7, 0), at(dc=1))
+    s_copy["far1"].wait_recv()
+    send_rows("far1s", 12, pair(6, 1), pair(7, 1), at(dc=1))
     pass_tables(1, (1,))
-    s_copy["far0"].wait_recv()
-    send_rows("far0s", 12, pair(4, 0), pair(5, 0), at(dc=1))
-    s_copy["far1"].wait_recv()
-    send_rows("far1s", 13, pair(4, 1), pair(5, 1), at(dc=1))
-    pack(4)
+    pack(6)
     for key in ("far0s", "far1s"):
         s_copy[key].wait_recv()
-    pack(5)
-    process(7)
-    process(1)
+    pack(7)
+    process(0, far)
+    process(7, far)
+    process(1, far)
     pass_tables(1, (2, 3))
     process(6)
     process(2)
-    loads["mortar"].wait()
-    process(0)
     pass_tables(2, (0,))
-    unpack(7, first=True)
-    pass_tables(2, (1,))
-    unpack(1)
+    unpack(0, first=True)
 
     loads["active"].wait()
     loads["multiplier"].wait()
     flag = column(active[...].astype(F32))
     count = jnp.sum(active[...].astype(F32), axis=1, keepdims=True)
     loads["inverse"].wait()
+    loads["scalars"].wait()
     for c in range(CORNERS):
         inverse_rows[c : c + 1, :] = inverse[pl.ds(corner_global_s[c], 1), :]
-    for copy in corner_copies:
-        copy.wait_recv()
+    await_bytes(corner_in.at[pl.ds(1, 3)], y_recv.at[2])
+    await_bytes(halo_facts, h_recv.at[1])
     own_nodes = None
     for i in range(NB + 2):
         facts = corner_in[i, CORNERS : CORNERS + 8, :] if i < NB else halo_facts[i - NB]
@@ -418,25 +411,32 @@
         ).astype(F32)
     patch_row3 = jnp.concatenate([patch_row] * 3, axis=1)
     back = (iota((PATCH, 3 * CORNERS), 0) == patch_row3).astype(F32).astype(BF16)
-    for copy in factor_copies:
-        copy.wait_recv()
+    await_bytes(factor.at[pl.ds(0, 3 * PATCH)], y_recv.at[0])
     own_factor.wait()
 
-    pass_tables(2, (2, 3))
-    process(5)
-    process(3)
+    def process_chunk(turn):
+        process(5, lo=orders[0][turn] * 128, width=128)
+        process(3, lo=orders[1][turn] * 128, width=128)
+
+    process_chunk(0)
+    pass_tables(2, (1,))
+    process_chunk(1)
+    unpack(7)
+    unpack(1)
+    pass_tables(2, (2,))
+    process_chunk(2)
     unpack(6)
+    pass_tables(2, (3,))
+    process_chunk(3)
     unpack(2)
     pass_tables(3, (0,))
-    process(4, 0)
-    unpack(0)
+    process(4, width=256, part=0)
     unpack(5)
     pass_tables(3, (1,))
-    process(4, 1)
+    process(4, lo=256, width=256, part=1)
     unpack(3)
     unpack(4, 0)
     unpack(4, 1)
-    blocks = [blocks_out[k] for k in range(4)]
 
     magnitude = jnp.sqrt(1.0 + (blocks[1] ** 2 + blocks[2] ** 2 + blocks[3] ** 2))
     residual = flag * blocks[0] / magnitude + (1.0 - flag) * multiplier[...]
@@ -462,28 +462,22 @@
         return min(step, around - step)
 
     def exchange(buffer, send_sem, recv_sem, group):
-        copies = []
-        for i, distance, there, to in sorted(group, key=lambda g: -g[1]):
-            copies.append(
-                send(buffer.at[0], buffer.at[there], send_sem.at[i], recv_sem.at[there], at(**to))
-            )
-        return copies
-
-    def gather(buffer, copies):
-        for copy in copies:
-            copy.wait_recv()
+        for _, there, to in sorted(group, key=lambda g: -g[0]):
+            send(buffer.at[0], buffer.at[there], send_sem.at[0], recv_sem.at[0], at(**to))
+
+    def gather(buffer, recv_sem):
+        await_bytes(buffer.at[pl.ds(1, 15)], recv_sem.at[0])
         total = buffer[0]
         for i in range(1, 16):
             total = total + buffer[i]
         return total
 
-    copies = exchange(
+    exchange(
         sum_a,
         a_send,
         a_recv,
         [
             (
-                dx * NB + dy,
                 hops(dx, NX) + hops(dy, NB),
                 ((-dx) % NX) * NB + (-dy) % NB,
                 dict(dx=dx, dy=dy),
@@ -491,40 +485,51 @@
             for dx, dy in group_a[1:]
         ],
     )
-    reduced_copies = [
-        send(reduced.at[own_rows], reduced.at[own_rows], y_send.at[1, dy], y_recv.at[1, dy], at(dy=dy))
-        for dy in (2, 1, 3)
-    ]
-    halo_copies = [
-        send(halo.at[2], halo.at[0], h_send.at[0], h_recv.at[0], behind),
-        send(halo.at[2], halo.at[1], h_send.at[1], h_recv.at[1], before),
-    ]
-    sum_b[0] = gather(sum_a, copies)
-    copies = exchange(
+    for dy in (2, 1, 3):
+        send(reduced.at[own_rows], reduced.at[own_rows], y_send.at[1], y_recv.at[1], at(dy=dy))
+    send(halo.at[2], halo.at[0], h_send.at[0], h_recv.at[0], behind)
+    send(halo.at[2], halo.at[1], h_send.at[0], h_recv.at[0], before)
+    for k in range(4):
+        blocks_out[:, k, :] = blocks[k]
+    sum_b[0] = gather(sum_a, a_recv)
+    exchange(
         sum_b,
         b_send,
         b_recv,
         [
-            (dz * 2 + dc, hops(dz, NZ) + 0.5 * dc, ((-dz) % NZ) * 2 + dc, dict(dz=dz, dc=dc))
+            (hops(dz, NZ) + 0.5 * dc, ((-dz) % NZ) * 2 + dc, dict(dz=dz, dc=dc))
             for dz, dc in group_b[1:]
         ],
     )
-    for copy in reduced_copies + halo_copies:
-        copy.wait_recv()
+    await_bytes(halo.at[pl.ds(0, 2)], h_recv.at[0])
+    await_bytes(reduced.at[pl.ds(0, 3 * PATCH)], y_recv.at[1])
     left = jnp.where(sub > 0, halo[0].astype(F32), 0.0)
     right = jnp.where(sub < 63, halo[1].astype(F32), 0.0)
     applied = dot(pieces[...], reduced[...])
     applied = applied[0:PATCH] + (applied[PATCH : 2 * PATCH] + applied[2 * PATCH :])
     image_out[...] = applied - 0.25 * (left + right)
-    total = gather(sum_b, copies)
+    total = gather(sum_b, b_recv)
     square_sum = total[:, COARSE : COARSE + 1]
     active_count = total[:, COARSE + 1 : COARSE + 2]
     scale = jnp.sqrt(active_count * float(NODE) / (square_sum + 1e-6))
     coarse = jnp.sum(inverse_rows[...] * total[:, :COARSE], axis=1, keepdims=True)
     correction = dot(back, jnp.concatenate(split3(coarse * own_nodes), axis=0))
     image_out[...] = scale * (image_out[...] + correction)
-    for copy in sends:
-        copy.wait_send()
+
+    for ref, sem in (
+        (table.at[pl.ds(1, 7)], t_send.at[0]),
+        (rows.at[pl.ds(1, 7)], s_send.at[0]),
+        (names.at[pl.ds(1, 7)], n_send.at[0]),
+        (product.at[:, pl.ds(1, 7)], r_send.at[0]),
+        (factor.at[pl.ds(0, 3 * PATCH)], y_send.at[0]),
+        (reduced.at[pl.ds(0, 3 * PATCH)], y_send.at[1]),
+        (corner_in.at[pl.ds(1, 3)], y_send.at[2]),
+        (halo.at[pl.ds(0, 2)], h_send.at[0]),
+        (halo_facts, h_send.at[1]),
+        (sum_a.at[pl.ds(1, 15)], a_send.at[0]),
+        (sum_b.at[pl.ds(1, 15)], b_send.at[0]),
+    ):
+        await_bytes(ref, sem)
 
 
 def body(
@@ -542,15 +547,14 @@
 ):
     vmem = pl.BlockSpec(memory_space=pltpu.VMEM)
     hbm = pl.BlockSpec(memory_space=pltpu.HBM)
-    smem = pl.BlockSpec(memory_space=pltpu.SMEM)
     dma = pltpu.SemaphoreType.DMA
-    blocks, image = pl.pallas_call(
+    return pl.pallas_call(
         kernel,
         out_shape=(
-            jax.ShapeDtypeStruct((4, PATCH, NODE), F32),
+            jax.ShapeDtypeStruct((PATCH, 4, NODE), F32),
             jax.ShapeDtypeStruct((PATCH, NODE), F32),
         ),
-        in_specs=[hbm] * 10 + [smem, hbm],
+        in_specs=[hbm] * 12,
         out_specs=(vmem, vmem),
         scratch_shapes=[
             pltpu.VMEM((4, PATCH, NODE), BF16),
@@ -575,23 +579,23 @@
             pltpu.VMEM((16, 1, MESSAGE), F32),
             pltpu.VMEM((COARSE, COARSE), F32),
             pltpu.VMEM((CORNERS, COARSE), F32),
+            dma((1,)),
             dma((2, 4, 4)),
-            dma((2, 4, 4)),
-            dma((14,)),
-            dma((14,)),
-            dma((8,)),
-            dma((8,)),
-            dma((9, 8)),
-            dma((9, 8)),
-            dma((3, 4)),
-            dma((3, 4)),
-            dma((4,)),
-            dma((4,)),
-            dma((16,)),
-            dma((16,)),
-            dma((16,)),
-            dma((16,)),
-            dma((12,)),
+            dma((1,)),
+            dma((13,)),
+            dma((1,)),
+            dma((1,)),
+            dma((1,)),
+            dma((9,)),
+            dma((3,)),
+            dma((3,)),
+            dma((2,)),
+            dma((2,)),
+            dma((1,)),
+            dma((1,)),
+            dma((1,)),
+            dma((1,)),
+            dma((13,)),
             pltpu.VMEM((PATCH, 4, NODE), BF16),
             pltpu.VMEM((3 * PATCH, NODE), BF16),
             pltpu.VMEM((NB, 24, 128), F32),
@@ -601,6 +605,8 @@
             pltpu.VMEM(((NB + 2) * CORNERS, COARSE), F32),
             pltpu.VMEM((2 * CORNERS, NODE), F32),
             pltpu.VMEM((2 * CORNERS, PATCH), BF16),
+            pltpu.SMEM((CORNERS,), I32),
+            pltpu.VMEM((4, PATCH, NODE), F32),
         ],
         compiler_params=pltpu.CompilerParams(
             collective_id=0, has_side_effects=True, vmem_limit_bytes=48 * 1024 * 1024
@@ -620,12 +626,11 @@
                 patch_coupling,
                 corner_local.reshape(1, CORNERS),
                 corner_global.reshape(1, CORNERS),
+                corner_global,
+                coarse_inverse,
             )
         ],
-        corner_global,
-        pltpu.with_memory_space_constraint(coarse_inverse, pltpu.HBM),
     )
-    return blocks.transpose(1, 0, 2), image
 
 
 def solution(mesh):

time: 77.5 us -> 71.1 us (0.917)
  Pallas kernels: 74.4 us -> 68.7 us
    pallas_call x1, Pallas kernels: 74.4 us -> 68.7 us  [body(): pl.pallas_call(kernel, out_shape=(jax.ShapeDtypeStruct((PATCH, 4, NODE),...]
where the time goes in v3:
time: 71.1 us; the launch traced here: 71 us
  Pallas kernels  68.7 us (97%)
  local copies, waits for them, and re-layouts  1.67 us (2%)
    pallas_call x1, Pallas kernels, body(): pl.pallas_call(kernel, out_shape=(jax.ShapeDtypeStruct((PATCH, 4, NODE),...  68.7 us
    unnamed x2, local copies, waits for them, and re-layouts  1.67 us

profile of v3, /device:TPU:1, one launch (start us, length us, event | category | flops | bytes accessed | tf_op | source)
XLA Modules:
  0.0 71.0 jit_solution(7637509481261000025)
XLA Ops:
  0.6 68.7 %newton_step.1 = (f32[128,4,512]{2,1,0:T(4,128)S(1)}, f32[128,512]{1,0:T(8,128)S(1)}) custom-call(bf16[128,4,512]{2,1,0:T(4,128)(2,1)} %slave_hbm.1, s32[2,128]{1,0:T(2,128)} %bitcast.6, f32[2,128]{1,0:T(2,128)} %bitcast.7, s32[1,128]{1,0:T(1,128)} %bitcast.8, f32[128,512]{1,0:T(8,128)} %multiplier_hbm.1, bf16[512,512]{1,0:T(8,128)(2,1)} %mortar.1, ...), custom_call_target="tpu_custom_call" | custom-call | tf_op jit(solution)/shard_map/newton_step/pallas_call | solution.py:551
  69.4 1.0 %copy.15 = f32[128,4,512]{2,1,0:T(4,128)} copy(f32[128,4,512]{2,1,0:T(4,128)S(1)} %get-tuple-element.4) | data formatting | bytes 2097152
  70.3 0.7 copy.16

commit v4 on v3

--- a/solution.py
+++ b/solution.py
@@ -107,6 +107,7 @@
     halo_patch,
     corner_global_s,
     blocks,
+    chooser,
 ):
     sub = lax.axis_index("sub")
     blk = lax.axis_index("blk")
@@ -418,40 +419,58 @@
         process(5, lo=orders[0][turn] * 128, width=128)
         process(3, lo=orders[1][turn] * 128, width=128)
 
+    for k in range(4):
+        for j in range(2):
+            chooser[(k * 2 + j) * PATCH : (k * 2 + j + 1) * PATCH] = (
+                (lanes + (4 * 256.0 - k * 8.0) == codes[j]).astype(F32).astype(BF16)
+            )
     process_chunk(0)
     pass_tables(2, (1,))
     process_chunk(1)
     unpack(7)
-    unpack(1)
     pass_tables(2, (2,))
     process_chunk(2)
-    unpack(6)
+    unpack(1)
     pass_tables(2, (3,))
     process_chunk(3)
-    unpack(2)
+    unpack(6)
     pass_tables(3, (0,))
     process(4, width=256, part=0)
-    unpack(5)
+    unpack(2)
     pass_tables(3, (1,))
     process(4, lo=256, width=256, part=1)
+    unpack(5)
     unpack(3)
-    unpack(4, 0)
-    unpack(4, 1)
-
-    magnitude = jnp.sqrt(1.0 + (blocks[1] ** 2 + blocks[2] ** 2 + blocks[3] ** 2))
-    residual = flag * blocks[0] / magnitude + (1.0 - flag) * multiplier[...]
-    rounded = residual.astype(BF16)
-    halo[2] = rounded
-    own_reduced = dot(rounded, factor[...]).astype(BF16)
+
+    summed, square = 0.0, 0.0
+    for part in range(2):
+        cols = pl.ds(part * 256, 256)
+        await_bytes(returned.at[4, pl.ds(1, 7), :, cols], r_recv.at[NZ if part else 4])
+        terms = dot(chooser[...], returned[4, :, :, cols].reshape(256, 256))
+        ready = []
+        for k in range(4):
+            total = blocks[k, :, cols]
+            for j in range(2):
+                total = total + weights[j] * terms[(k * 2 + j) * PATCH : (k * 2 + j + 1) * PATCH]
+            blocks[k, :, cols] = total
+            ready.append(total)
+        magnitude = jnp.sqrt(1.0 + (ready[1] ** 2 + ready[2] ** 2 + ready[3] ** 2))
+        residual = flag * ready[0] / magnitude + (1.0 - flag) * multiplier[:, cols]
+        halo[2, :, cols] = residual.astype(BF16)
+        summed = summed + dot(residual.astype(BF16), factor[cols, :])
+        square = square + jnp.sum(residual * residual, axis=0, keepdims=True)
+    own_reduced = summed.astype(BF16)
     reduced[own_rows, :] = own_reduced
+    for dy in (2, 1, 3):
+        send(reduced.at[own_rows], reduced.at[own_rows], y_send.at[1], y_recv.at[1], at(dy=dy))
 
     picked = lax.dot_general(
         at_node[...], own_reduced, (((1,), (1,)), ((), ())), preferred_element_type=F32
     )
     values = jnp.sum(picked * corner_in[:, 0:CORNERS, :].reshape(64, PATCH), axis=1, keepdims=True)
-    beside = jnp.sum(dot(halo_patch[...], rounded) * halo_node[...], axis=1, keepdims=True)
+    beside = jnp.sum(dot(halo_patch[...], halo[2]) * halo_node[...], axis=1, keepdims=True)
     values = jnp.concatenate([values, beside], axis=0)
-    square = jnp.sum(jnp.sum(residual * residual, axis=0, keepdims=True), axis=1, keepdims=True)
+    square = jnp.sum(square, axis=1, keepdims=True)
     lane = iota((1, 128), 1)
     extra = jnp.where(lane == 0, square, jnp.where(lane == 1, count, 0.0))
     sum_a[0] = jnp.concatenate(
@@ -477,16 +496,10 @@
         a_send,
         a_recv,
         [
-            (
-                hops(dx, NX) + hops(dy, NB),
-                ((-dx) % NX) * NB + (-dy) % NB,
-                dict(dx=dx, dy=dy),
-            )
-            for dx, dy in group_a[1:]
+            (hops(dz, NZ) + 0.5 * dc, ((-dz) % NZ) * 2 + dc, dict(dz=dz, dc=dc))
+            for dz, dc in group_b[1:]
         ],
     )
-    for dy in (2, 1, 3):
-        send(reduced.at[own_rows], reduced.at[own_rows], y_send.at[1], y_recv.at[1], at(dy=dy))
     send(halo.at[2], halo.at[0], h_send.at[0], h_recv.at[0], behind)
     send(halo.at[2], halo.at[1], h_send.at[0], h_recv.at[0], before)
     for k in range(4):
@@ -497,8 +510,12 @@
         b_send,
         b_recv,
         [
-            (hops(dz, NZ) + 0.5 * dc, ((-dz) % NZ) * 2 + dc, dict(dz=dz, dc=dc))
-            for dz, dc in group_b[1:]
+            (
+                hops(dx, NX) + hops(dy, NB),
+                ((-dx) % NX) * NB + (-dy) % NB,
+                dict(dx=dx, dy=dy),
+            )
+            for dx, dy in group_a[1:]
         ],
     )
     await_bytes(halo.at[pl.ds(0, 2)], h_recv.at[0])
@@ -607,6 +624,7 @@
             pltpu.VMEM((2 * CORNERS, PATCH), BF16),
             pltpu.SMEM((CORNERS,), I32),
             pltpu.VMEM((4, PATCH, NODE), F32),
+            pltpu.VMEM((8 * PATCH, 256), BF16),
         ],
         compiler_params=pltpu.CompilerParams(
             collective_id=0, has_side_effects=True, vmem_limit_bytes=48 * 1024 * 1024

time: 71.1 us -> 68.9 us (0.969)
  Pallas kernels: 68.7 us -> 66.4 us
    pallas_call x1, Pallas kernels: 68.7 us -> 66.4 us  [body(): pl.pallas_call(kernel, out_shape=(jax.ShapeDtypeStruct((PATCH, 4, NODE),...]
where the time goes in v4:
time: 68.9 us; the launch traced here: 68.8 us
  Pallas kernels  66.4 us (96%)
  local copies, waits for them, and re-layouts  1.67 us (2%)
    pallas_call x1, Pallas kernels, body(): pl.pallas_call(kernel, out_shape=(jax.ShapeDtypeStruct((PATCH, 4, NODE),...  66.4 us
    unnamed x2, local copies, waits for them, and re-layouts  1.67 us

profile of v4, /device:TPU:1, one launch (start us, length us, event | category | flops | bytes accessed | tf_op | source)
XLA Modules:
  0.0 68.8 jit_solution(17448059129278614322)
XLA Ops:
  0.6 66.4 %newton_step.1 = (f32[128,4,512]{2,1,0:T(4,128)S(1)}, f32[128,512]{1,0:T(8,128)S(1)}) custom-call(bf16[128,4,512]{2,1,0:T(4,128)(2,1)} %slave_hbm.1, s32[2,128]{1,0:T(2,128)} %bitcast.6, f32[2,128]{1,0:T(2,128)} %bitcast.7, s32[1,128]{1,0:T(1,128)} %bitcast.8, f32[128,512]{1,0:T(8,128)} %multiplier_hbm.1, bf16[512,512]{1,0:T(8,128)(2,1)} %mortar.1, ...), custom_call_target="tpu_custom_call" | custom-call | tf_op jit(solution)/shard_map/newton_step/pallas_call | solution.py:568
  67.1 1.0 %copy.15 = f32[128,4,512]{2,1,0:T(4,128)} copy(f32[128,4,512]{2,1,0:T(4,128)S(1)} %get-tuple-element.4) | data formatting | bytes 2097152
  68.1 0.7 %copy.16 = f32[128,512]{1,0:T(8,128)} copy(f32[128,512]{1,0:T(8,128)S(1)} %get-tuple-element.5) | data formatting | bytes 524288

commit v5 on v4

--- a/solution.py
+++ b/solution.py
@@ -115,6 +115,7 @@
     z = (sub // 2) % NZ
     core = sub % 2
 
+    @functools.cache
     def at(dx=0, dz=0, dc=0, dy=0):
         xx = (x + dx) % NX
         zz = (z + dz) % NZ
@@ -139,11 +140,11 @@
     for i, (name, src, dst) in enumerate(
         (
             ("masters", masters_hbm, masters),
+            ("mortar", mortar, table.at[0]),
             ("scalars", corner_global_hbm1, corner_global_s),
             ("slave", slave_hbm, slave_raw),
             ("schur", schur_hbm, schur),
             ("weight", weight_hbm, weight),
-            ("mortar", mortar, table.at[0]),
             ("active", active_hbm, active),
             ("local", corner_local_hbm, corner_local),
             ("global", corner_global_hbm, corner_global),
@@ -154,26 +155,23 @@
         loads[name] = pltpu.make_async_copy(src, dst, local_sem.at[i])
         loads[name].start()
 
-    row_peers = [(dx, dc) for dx in range(NX) for dc in range(2)]
+    row_peers = [(0, 0)] + [(dx, dc) for dx in (2, 1, 3) for dc in (1, 0)] + [(0, 1)]
     group_a = [(dx, dy) for dx in range(NX) for dy in range(NB)]
     group_b = [(dz, dc) for dz in range(NZ) for dc in range(2)]
     greet = {(dx, 0, dc, 0) for dx, dc in row_peers}
-    greet |= {(dx, 0, 0, dy) for dx, dy in group_a}
+    greet |= {(0, 0, 0, dy) for dy in range(NB)}
     greet |= {(0, dz, 0, 0) for dz in (1, NZ - 1)}
     greet = sorted(greet - {(0, 0, 0, 0)})
     before, behind = ((sub + 63) % 64, blk), ((sub + 1) % 64, blk)
     barrier = pltpu.get_barrier_semaphore()
     for dx, dz, dc, dy in greet:
         pl.semaphore_signal(barrier, inc=1, device_id=at(dx, dz, dc, dy), device_id_type=MESH)
-    for neighbour in (before, behind):
-        pl.semaphore_signal(barrier, inc=1, device_id=neighbour, device_id_type=MESH)
     loads["masters"].wait()
     names[0] = jnp.zeros((8, PATCH), I32)
     names[0, 0:2, :] = masters[...]
-    pl.semaphore_wait(barrier, len(greet) + 2)
+    pl.semaphore_wait(barrier, len(greet))
 
     orders = ((0, 2, 1, 3), (1, 3, 0, 2))
-    tables = {}
 
     def chunk(ref, q):
         return ref.at[:, pl.ds(q * 128, 128)]
@@ -181,23 +179,24 @@
     def send_table(way, step, q):
         slot = (-step) % NZ if way == 0 else step
         land = (-step - 1) % NZ if way == 0 else step + 1
-        src = mortar if step == 0 else table.at[slot]
-        tables[way, step, q] = send(
+        src = table.at[slot]
+        send(
             chunk(src, q),
             chunk(table.at[land], q),
             t_send.at[0],
-            t_recv.at[way, step, q],
+            t_recv.at[step, orders[way].index(q)],
             at(dz=1 if way == 0 else -1),
         )
 
     def pass_tables(step, turns):
         for turn in turns:
+            await_bytes(table.at[step + 1, :, pl.ds(0, 256)], t_recv.at[step, turn])
             for way in (0, 1):
                 q = orders[way][turn]
-                tables[way, step, q].wait_recv()
                 if step < 2 or (step == 2 and turn < 2):
                     send_table(way, step + 1, q)
 
+    loads["mortar"].wait()
     for turn in range(4):
         for way in (0, 1):
             send_table(way, 0, orders[way][turn])
@@ -249,17 +248,6 @@
     for i in range(NB):
         corner_out[i] = jnp.concatenate([corner_rows[:, i * 128 : (i + 1) * 128], facts], axis=0)
     corner_in[0] = corner_out[blk]
-    for dy in range(1, NB):
-        send(
-            corner_out.at[(blk + dy) % NB],
-            corner_in.at[(-dy) % NB],
-            y_send.at[2],
-            y_recv.at[2],
-            at(dy=dy),
-        )
-    facts_ref = corner_out.at[0, pl.ds(CORNERS, 8)]
-    send(facts_ref, halo_facts.at[0], h_send.at[1], h_recv.at[1], behind)
-    send(facts_ref, halo_facts.at[1], h_send.at[1], h_recv.at[1], before)
 
     strict = (iota((256, 256), 0) < iota((256, 256), 1)).astype(F32).astype(BF16)
 
@@ -279,6 +267,14 @@
     weights = [column(weight[j : j + 1, :]) for j in range(2)]
 
     await_bytes(names.at[pl.ds(1, 7)], n_recv.at[0])
+    for dy in range(1, NB):
+        send(
+            corner_out.at[(blk + dy) % NB],
+            corner_in.at[(-dy) % NB],
+            y_send.at[2],
+            y_recv.at[2],
+            at(dy=dy),
+        )
     mine = ((x * NZ + (z + iota((8, 256), 0)) % NZ) * 2 + core).astype(I32)
     named = jnp.concatenate(
         [(entries(names[slot]) == mine).astype(F32) for slot in range(8)], axis=0
@@ -358,9 +354,11 @@
     for key in ("down0s", "down1s"):
         s_copy[key].wait_recv()
     pack(3)
-    loads["mortar"].wait()
     process(0, near)
     pass_tables(1, (0,))
+    facts_ref = corner_out.at[0, pl.ds(CORNERS, 8)]
+    send(facts_ref, halo_facts.at[0], h_send.at[1], h_recv.at[1], behind)
+    send(facts_ref, halo_facts.at[1], h_send.at[1], h_recv.at[1], before)
     process(7, near)
     process(1, near)
     s_copy["far0"].wait_recv()
@@ -597,7 +595,7 @@
             pltpu.VMEM((COARSE, COARSE), F32),
             pltpu.VMEM((CORNERS, COARSE), F32),
             dma((1,)),
-            dma((2, 4, 4)),
+            dma((4, 4)),
             dma((1,)),
             dma((13,)),
             dma((1,)),

time: 68.9 us -> 68.2 us (0.990)
  no operation moved by 1% of the time
where the time goes in v5:
time: 68.2 us; the launch traced here: 68.1 us
  Pallas kernels  65.8 us (96%)
  local copies, waits for them, and re-layouts  1.67 us (2%)
    pallas_call x1, Pallas kernels, body(): pl.pallas_call(kernel, out_shape=(jax.ShapeDtypeStruct((PATCH, 4, NODE),...  65.8 us
    unnamed x2, local copies, waits for them, and re-layouts  1.67 us

profile of v5, /device:TPU:1, one launch (start us, length us, event | category | flops | bytes accessed | tf_op | source)
XLA Modules:
  0.0 68.1 jit_solution(5178212972899621124)
XLA Ops:
  0.6 65.8 %newton_step.1 = (f32[128,4,512]{2,1,0:T(4,128)S(1)}, f32[128,512]{1,0:T(8,128)S(1)}) custom-call(bf16[128,4,512]{2,1,0:T(4,128)(2,1)} %slave_hbm.1, s32[2,128]{1,0:T(2,128)} %bitcast.6, f32[2,128]{1,0:T(2,128)} %bitcast.7, s32[1,128]{1,0:T(1,128)} %bitcast.8, f32[128,512]{1,0:T(8,128)} %multiplier_hbm.1, bf16[512,512]{1,0:T(8,128)(2,1)} %mortar.1, ...), custom_call_target="tpu_custom_call" | custom-call | tf_op jit(solution)/shard_map/newton_step/pallas_call | solution.py:566
  66.4 1.0 %copy.15 = f32[128,4,512]{2,1,0:T(4,128)} copy(f32[128,4,512]{2,1,0:T(4,128)S(1)} %get-tuple-element.4) | data formatting | bytes 2097152
  67.4 0.7 %copy.16 = f32[128,512]{1,0:T(8,128)} copy(f32[128,512]{1,0:T(8,128)S(1)} %get-tuple-element.5) | data formatting | bytes 524288

commit v6 on v5

--- a/solution.py
+++ b/solution.py
@@ -459,8 +459,10 @@
         square = square + jnp.sum(residual * residual, axis=0, keepdims=True)
     own_reduced = summed.astype(BF16)
     reduced[own_rows, :] = own_reduced
-    for dy in (2, 1, 3):
-        send(reduced.at[own_rows], reduced.at[own_rows], y_send.at[1], y_recv.at[1], at(dy=dy))
+    for part in range(2):
+        piece = reduced.at[own_rows, pl.ds(part * 256, 256)]
+        for dy in (2, 1, 3):
+            send(piece, piece, y_send.at[1], y_recv.at[1 + 2 * part], at(dy=dy))
 
     picked = lax.dot_general(
         at_node[...], own_reduced, (((1,), (1,)), ((), ())), preferred_element_type=F32
@@ -517,12 +519,15 @@
         ],
     )
     await_bytes(halo.at[pl.ds(0, 2)], h_recv.at[0])
-    await_bytes(reduced.at[pl.ds(0, 3 * PATCH)], y_recv.at[1])
     left = jnp.where(sub > 0, halo[0].astype(F32), 0.0)
     right = jnp.where(sub < 63, halo[1].astype(F32), 0.0)
-    applied = dot(pieces[...], reduced[...])
-    applied = applied[0:PATCH] + (applied[PATCH : 2 * PATCH] + applied[2 * PATCH :])
-    image_out[...] = applied - 0.25 * (left + right)
+    image_out[...] = -0.25 * (left + right)
+    for part in range(2):
+        cols = pl.ds(part * 256, 256)
+        await_bytes(reduced.at[pl.ds(0, 3 * PATCH), cols], y_recv.at[1 + 2 * part])
+        applied = dot(pieces[...], reduced[:, cols])
+        applied = applied[0:PATCH] + (applied[PATCH : 2 * PATCH] + applied[2 * PATCH :])
+        image_out[:, cols] = applied + image_out[:, cols]
     total = gather(sum_b, b_recv)
     square_sum = total[:, COARSE : COARSE + 1]
     active_count = total[:, COARSE + 1 : COARSE + 2]
@@ -603,7 +608,7 @@
             dma((1,)),
             dma((9,)),
             dma((3,)),
-            dma((3,)),
+            dma((4,)),
             dma((2,)),
             dma((2,)),
             dma((1,)),

time: 68.2 us -> 68.2 us (level)
  no operation moved by 1% of the time
where the time goes in v6:
time: 68.2 us; the launch traced here: 68.1 us
  Pallas kernels  65.8 us (96%)
  local copies, waits for them, and re-layouts  1.67 us (2%)
    pallas_call x1, Pallas kernels, body(): pl.pallas_call(kernel, out_shape=(jax.ShapeDtypeStruct((PATCH, 4, NODE),...  65.8 us
    unnamed x2, local copies, waits for them, and re-layouts  1.67 us

profile of v6, /device:TPU:1, one launch (start us, length us, event | category | flops | bytes accessed | tf_op | source)
XLA Modules:
  0.0 68.1 jit_solution(14566800347652420368)
XLA Ops:
  0.6 65.8 %newton_step.1 = (f32[128,4,512]{2,1,0:T(4,128)S(1)}, f32[128,512]{1,0:T(8,128)S(1)}) custom-call(bf16[128,4,512]{2,1,0:T(4,128)(2,1)} %slave_hbm.1, s32[2,128]{1,0:T(2,128)} %bitcast.6, f32[2,128]{1,0:T(2,128)} %bitcast.7, s32[1,128]{1,0:T(1,128)} %bitcast.8, f32[128,512]{1,0:T(8,128)} %multiplier_hbm.1, bf16[512,512]{1,0:T(8,128)(2,1)} %mortar.1, ...), custom_call_target="tpu_custom_call" | custom-call | tf_op jit(solution)/shard_map/newton_step/pallas_call | solution.py:571
  66.5 1.0 %copy.15 = f32[128,4,512]{2,1,0:T(4,128)} copy(f32[128,4,512]{2,1,0:T(4,128)S(1)} %get-tuple-element.4) | data formatting | bytes 2097152
  67.4 0.7 %copy.16 = f32[128,512]{1,0:T(8,128)} copy(f32[128,512]{1,0:T(8,128)S(1)} %get-tuple-element.5) | data formatting | bytes 524288
